TPU v7x, 256 devices: a whole 4x4x8 slice. The times are simulated.
256 devices in a mesh: dp: 8 (over z_hi, x), space: 32 (over y, z_lo, core).
Axes of the slice: x: 4, y: 4, z: 8 (z_hi: 2, z_lo: 4; z = z_hi * 4 + z_lo), core: 2. Of those that a mesh axis runs over, the one named last changes fastest.
Arguments:
- inputs: bfloat16 [16, 96, 180, 768], P('dp', 'space'), may hold values from -6 to 6
- cotangent: bfloat16 [16, 96, 180, 768], P('dp', 'space'), may hold values from -6 to 6
- kept_modes: int32 [8, 96, 96], P(None, None, 'space'), may hold values 0 or 1
- pad_rows: int32 [1], replicated, may hold values from 0 to 8
- weight_one: bfloat16 [2, 8, 96, 96], replicated, may hold values from -0.4375 to 0.4375
- bias_one: float32 [2, 8, 96], replicated, may hold values from -3 to 3
- weight_two: bfloat16 [2, 8, 96, 96], replicated, may hold values from -0.4375 to 0.4375
- bias_two: float32 [2, 8, 96], replicated, may hold values from -2 to 2
Outputs:
- output: bfloat16 [16, 96, 180, 768], P('dp', 'space')
- grad_in: bfloat16 [16, 96, 180, 768], P('dp', 'space')
- grad_weight_one: float32 [2, 8, 96, 96], replicated
- grad_bias_one: float32 [2, 8, 96], replicated
- grad_weight_two: float32 [2, 8, 96, 96], replicated
- grad_bias_two: float32 [2, 8, 96], replicated
Inputs may be any that keep to these rules, and one draw needn't show every extreme that they name: kept_modes holds only 0 and 1.
All inputs are finite; a program needn't handle non-finite values. No bound on the sum of `kept_modes` on one device may be relied on, other than what follows from the above.
Results may differ from a plain program's by a relative error of at most 0.012.
Values may be sent and summed in bfloat16 or wider, within the bound.
A program may use at most 128 MiB of HBM per device.

v0:
```python
import jax
import jax.numpy as jnp
from jax import lax
from jax.sharding import PartitionSpec as P

shrink = 0.25
gelu_scale = 0.7978845608028654
gelu_cubic = 0.044715


def gelu_value(value):
    return 0.5 * value * (1.0 + jnp.tanh(gelu_scale * (value + gelu_cubic * value * value * value)))


def gelu_slope(value):
    tangent = jnp.tanh(gelu_scale * (value + gelu_cubic * value * value * value))
    inner = gelu_scale * (1.0 + 3.0 * gelu_cubic * value * value)
    return 0.5 * (1.0 + tangent) + 0.5 * value * (1.0 - tangent * tangent) * inner


def longitude_tables(width, padded):
    wavenum = jnp.arange(padded, dtype=jnp.int32)[:, None]
    column = jnp.arange(width, dtype=jnp.int32)[None, :]
    phase = 2.0 * jnp.pi / width * (wavenum * column % width).astype(jnp.float32)
    scaling = (wavenum < width // 2 + 1).astype(jnp.float32) / jnp.sqrt(jnp.float32(width))
    double = jnp.where(jnp.logical_or(wavenum == 0, 2 * wavenum == width), 1.0, 2.0).astype(
        jnp.float32
    )
    cosine = jnp.cos(phase) * scaling
    sine = jnp.sin(phase) * scaling
    forward = jnp.concatenate([cosine, -sine], 0).astype(jnp.bfloat16)
    inverse = jnp.concatenate([double * cosine, -double * sine], 0).astype(jnp.bfloat16)
    return (forward, inverse)


def latitude_table(length, sign):
    row = jnp.arange(length, dtype=jnp.int32)[:, None]
    column = jnp.arange(length, dtype=jnp.int32)[None, :]
    phase = 2.0 * jnp.pi / length * (row * column % length).astype(jnp.float32)
    scaling = 1.0 / jnp.sqrt(jnp.float32(length))
    cosine = jnp.cos(phase) * scaling
    sine = sign * jnp.sin(phase) * scaling
    upper = jnp.stack([cosine, sine], -1)
    lower = jnp.stack([-sine, cosine], -1)
    return jnp.stack([upper, lower], 0).astype(jnp.bfloat16)


def complex_matrix(weights):
    real_part, imag_part = (weights[0], weights[1])
    from_real = jnp.stack([real_part, imag_part], 2)
    from_imag = jnp.stack([-imag_part, real_part], 2)
    return jnp.stack([from_real, from_imag], 1)


def weight_grad(big):
    real_part = big[:, 0, :, 0, :] + big[:, 1, :, 1, :]
    imag_part = big[:, 0, :, 1, :] - big[:, 1, :, 0, :]
    return jnp.stack([real_part, imag_part], 0)


def on_device(inputs, cotangent, kept_modes, pad_rows, weight_one, bias_one, weight_two, bias_two):
    batch, rows, width, chans = inputs.shape
    blocks_count, size_block = (weight_one.shape[1], weight_one.shape[2])
    parts = lax.axis_size("space")
    local_modes = kept_modes.shape[2]
    padded = local_modes * parts
    full_rows = kept_modes.shape[1]
    forward_lon, inverse_lon = longitude_tables(width, padded)
    lat_forward = latitude_table(full_rows, 1.0)
    lat_inverse = latitude_table(full_rows, -1.0)
    big_one = complex_matrix(weight_one)
    big_two = complex_matrix(weight_two)
    row_ids = lax.axis_index("space") * rows + jnp.arange(rows, dtype=jnp.int32)
    valid = (row_ids < full_rows - pad_rows[0]).astype(jnp.bfloat16)[None, :, None, None]
    mode_ids = lax.axis_index("space") * local_modes + jnp.arange(local_modes, dtype=jnp.int32)
    keep = (
        kept_modes.astype(jnp.float32)
        * (mode_ids < width // 2 + 1).astype(jnp.float32)[None, None, :]
    )
    keep = jnp.transpose(keep, (1, 2, 0))[None, None, :, :, :, None]

    def to_modes(field, table):
        spec = jnp.einsum("bhwc,kw->bhkc", field, table, preferred_element_type=jnp.float32)
        return spec.astype(jnp.bfloat16).reshape(field.shape[0], rows, 2, padded, chans)

    def to_field(piece, table):
        flat = piece.reshape(piece.shape[0], rows, 2 * padded, chans)
        return jnp.einsum("bhkc,kw->bhwc", flat, table, preferred_element_type=jnp.float32)

    def spectral(piece):
        return jnp.einsum(
            "pqhr,bhrkc->bpqkc", lat_forward, piece, preferred_element_type=jnp.float32
        )

    def unspectral(piece):
        result = jnp.einsum(
            "phqr,brqkc->bhpkc", lat_inverse, piece, preferred_element_type=jnp.float32
        )
        return result.astype(jnp.bfloat16)

    masked = inputs * valid
    gated = cotangent * valid
    spectrum = spectral(
        lax.all_to_all(
            to_modes(masked, forward_lon), "space", split_axis=3, concat_axis=1, tiled=True
        )
    ).astype(jnp.bfloat16)
    shape_six = (batch, 2, full_rows, local_modes, blocks_count, size_block)
    blocks = spectrum.reshape(shape_six)
    pre_one = (
        jnp.einsum("brhknc,nrcpd->bphknd", blocks, big_one, preferred_element_type=jnp.float32)
        + bias_one[None, :, None, None]
    )
    hidden = gelu_value(pre_one).astype(jnp.bfloat16)
    pre_two = (
        jnp.einsum("brhknc,nrcpd->bphknd", hidden, big_two, preferred_element_type=jnp.float32)
        + bias_two[None, :, None, None]
    )
    tangent = jnp.tanh(pre_two / shrink)
    shrunk = pre_two - shrink * tangent
    filtered = (shrunk * keep).astype(jnp.bfloat16).reshape(batch, 2, full_rows, local_modes, chans)
    back_lat = unspectral(filtered)
    field = to_field(
        lax.all_to_all(back_lat, "space", split_axis=1, concat_axis=3, tiled=True), inverse_lon
    )
    output = ((inputs + field) * valid).astype(jnp.bfloat16)
    d_filtered = spectral(
        lax.all_to_all(
            to_modes(gated, inverse_lon), "space", split_axis=3, concat_axis=1, tiled=True
        )
    )
    d_two = (d_filtered.reshape(shape_six) * keep * (tangent * tangent)).astype(jnp.bfloat16)
    grad_two = weight_grad(
        jnp.einsum("brhknc,bphknd->nrcpd", hidden, d_two, preferred_element_type=jnp.float32)
    )
    bias_grad_two = jnp.sum(d_two.astype(jnp.float32), axis=(0, 2, 3))
    d_hidden = jnp.einsum(
        "bphknd,nrcpd->brhknc", d_two, big_two, preferred_element_type=jnp.float32
    )
    d_one = (d_hidden * gelu_slope(pre_one)).astype(jnp.bfloat16)
    grad_one = weight_grad(
        jnp.einsum("brhknc,bphknd->nrcpd", blocks, d_one, preferred_element_type=jnp.float32)
    )
    bias_grad_one = jnp.sum(d_one.astype(jnp.float32), axis=(0, 2, 3))
    grad_one, bias_grad_one, grad_two, bias_grad_two = lax.psum(
        (grad_one, bias_grad_one, grad_two, bias_grad_two), ("dp", "space")
    )
    d_spec = jnp.einsum("bphknd,nrcpd->brhknc", d_one, big_one, preferred_element_type=jnp.float32)
    d_spec = d_spec.astype(jnp.bfloat16).reshape(batch, 2, full_rows, local_modes, chans)
    d_lat = unspectral(d_spec)
    d_field = to_field(
        lax.all_to_all(d_lat, "space", split_axis=1, concat_axis=3, tiled=True), forward_lon
    )
    grad_in = (gated + d_field * valid).astype(jnp.bfloat16)
    scaling = 1.0 / (lax.axis_size("dp") * batch * full_rows)
    return (
        output,
        grad_in,
        grad_one * scaling,
        bias_grad_one * scaling,
        grad_two * scaling,
        bias_grad_two * scaling,
    )


def solution(mesh):
    placed = (
        P("dp", "space", None, None),
        P("dp", "space", None, None),
        P(None, None, "space"),
        P(),
        P(),
        P(),
        P(),
        P(),
    )
    return jax.shard_map(
        on_device,
        mesh=mesh,
        in_specs=placed,
        out_specs=(P("dp", "space", None, None), P("dp", "space", None, None), P(), P(), P(), P()),
        check_vma=False,
    )
```

profile of v0, /device:TPU:1, one launch (start us, length us, event | category | flops | bytes accessed | tf_op | source)
XLA Modules:
  0.0 501.2 jit_solution(9964669041356544957)
XLA Ops:
  11.8 3.1 copy.104
  14.8 10.2 %all-to-all-start.2 = ((bf16[2,3,2,96,768]{4,2,1,0,3:T(2,128)(2,1)}), bf16[2,3,2,96,768]{4,2,1,0,3:T(2,128)(2,1)S(1)}, u32[]{:S(2)}, u32[]{:S(2)}) async-start(bf16[2,3,2,96,768]{4,2,1,0,3:T(2,128)(2,1)} %copy.104), calls=%async_computation.2 | async-start | bytes 3538944 | tf_op jit(solution)/shard_map/all_to_all | solution.py:128
  27.3 3.1 copy.88
  30.4 37.6 %all-to-all-done.2 = bf16[2,3,2,96,768]{4,2,1,0,3:T(2,128)(2,1)S(1)} async-done(((bf16[2,3,2,96,768]{4,2,1,0,3:T(2,128)(2,1)}), bf16[2,3,2,96,768]{4,2,1,0,3:T(2,128)(2,1)S(1)}, u32[]{:S(2)}, u32[]{:S(2)}) %all-to-all-start.2) | async-done | bytes 1769504 | tf_op jit(solution)/shard_map/all_to_all | solution.py:128
  68.0 5.7 %all-to-all-start = ((bf16[2,3,2,96,768]{4,2,1,0,3:T(2,128)(2,1)}), bf16[2,3,2,96,768]{4,2,1,0,3:T(2,128)(2,1)}, u32[]{:S(2)}, u32[]{:S(2)}) async-start(bf16[2,3,2,96,768]{4,2,1,0,3:T(2,128)(2,1)} %copy.88), calls=%async_computation | async-start | bytes 3538944 | tf_op jit(solution)/shard_map/all_to_all | solution.py:104
  79.9 3.7 reshape.306
  83.6 33.0 %all-to-all-done = bf16[2,3,2,96,768]{4,2,1,0,3:T(2,128)(2,1)} async-done(((bf16[2,3,2,96,768]{4,2,1,0,3:T(2,128)(2,1)}), bf16[2,3,2,96,768]{4,2,1,0,3:T(2,128)(2,1)}, u32[]{:S(2)}, u32[]{:S(2)}) %all-to-all-start) | async-done | bytes 1769504 | tf_op jit(solution)/shard_map/all_to_all | solution.py:104
  121.3 4.1 reshape.267
  128.0 6.8 %convert_reduce_fusion = (f32[2,8,96]{2,0,1:T(2,128)S(1)}, bf16[2,2,96,3,8,96]{5,2,3,0,1,4:T(8,128)(2,1)S(1)}, bf16[2,2,96,3,8,96]{5,2,3,0,1,4:T(8,128)(2,1)}) fusion(f32[2,8,96]{2,0,1:T(2,128)S(1)} %copy.95, f32[96,3,8]{0,1,2:T(4,128)S(1)} %copy-done.24, f32[2,2,96,3,8,96]{5,4,2,1,3,0:T(8,128)} %reshape.306, ...), kind=kOutput, calls=%fused_computation.16 | convolution fusion | flops 351533568 | bytes 9458688 | tf_op jit(solution)/shard_map/brhknc,nrcpd->bphknd/dot_general | solution.py:116
  134.8 4.1 convert_reduce_fusion.1
  142.8 4.5 copy.184
  147.3 4.7 reshape.296
  154.1 3.0 copy.116
  157.2 5.4 %all-to-all-start.3 = ((bf16[2,96,2,3,768]{4,2,3,0,1:T(2,128)(2,1)}), bf16[2,96,2,3,768]{4,2,3,0,1:T(2,128)(2,1)}, u32[]{:S(2)}, u32[]{:S(2)}) async-start(bf16[2,96,2,3,768]{4,2,3,0,1:T(2,128)(2,1)} %copy.116), calls=%async_computation.3 | async-start | bytes 3538944 | tf_op jit(solution)/shard_map/all_to_all | solution.py:152
  162.6 4.6 copy.169
  167.2 4.7 reshape.284
  174.0 3.1 copy.99
  177.2 28.4 %all-to-all-done.3 = bf16[2,96,2,3,768]{4,2,3,0,1:T(2,128)(2,1)} async-done(((bf16[2,96,2,3,768]{4,2,3,0,1:T(2,128)(2,1)}), bf16[2,96,2,3,768]{4,2,3,0,1:T(2,128)(2,1)}, u32[]{:S(2)}, u32[]{:S(2)}) %all-to-all-start.3) | async-done | bytes 1769504 | tf_op jit(solution)/shard_map/all_to_all | solution.py:152
  205.5 5.0 all-to-all-start.1
  210.5 3.3 fusion.55
  217.8 82.1 %all-reduce = (f32[2,8,96]{2,0,1:T(2,128)S(1)}, f32[2,8,96]{2,0,1:T(2,128)S(1)}) all-reduce(f32[2,8,96]{2,0,1:T(2,128)S(1)} %get-tuple-element.51, f32[2,8,96]{2,0,1:T(2,128)S(1)} %get-tuple-element.28), channel_id=1, replica_groups=mesh['dp'=8,'space'=32] {'dp','space'}, use_global_device_ids=true, to_apply=%region_2.3 | all-reduce | flops 3072 | bytes 24576 | tf_op jit(solution)/shard_map/psum | solution.py:145
  301.2 176.2 %all-reduce.4.cloned.1.call-done = (f32[2,8,96,96]{3,2,1,0:T(8,128)}, f32[2,8,96,96]{3,2,1,0:T(8,128)}) async-done(((f32[2,8,96,96]{3,2,1,0:T(8,128)}, f32[2,8,96,96]{3,2,1,0:T(8,128)}), (f32[2,8,96,96]{3,2,1,0:T(8,128)}, f32[2,8,96,96]{3,2,1,0:T(8,128)})) %all-reduce.4.cloned.1.call-update) | async-done | bytes 1179664 | tf_op jit(solution)/shard_map/psum | solution.py:145
  481.7 2.8 copy.118
  487.9 3.0 copy.101
  (114 shorter events, 43.5 us)
Async XLA Ops:
  8.4 16.6 %copy-start.29 = (bf16[3]{0:T(256)(128)(2,1)}, bf16[3]{0:T(256)(128)(2,1)S(1)}, u32[]{:S(2)}) copy-start(bf16[3]{0:T(256)(128)(2,1)S(1)} %get-tuple-element.31) | copy-start | bytes 22
  8.9 16.1 %copy-start.20 = (bf16[96,180]{0,1:T(8,128)(2,1)}, bf16[96,180]{0,1:T(8,128)(2,1)S(1)}, u32[]{:S(2)}) copy-start(bf16[96,180]{0,1:T(8,128)(2,1)S(1)} %get-tuple-element.49) | copy-start | bytes 103684
  8.9 16.1 %copy-start.22 = (bf16[96,180]{0,1:T(8,128)(2,1)}, bf16[96,180]{0,1:T(8,128)(2,1)S(1)}, u32[]{:S(2)}) copy-start(bf16[96,180]{0,1:T(8,128)(2,1)S(1)} %get-tuple-element.50) | copy-start | bytes 103684
  14.8 53.2 %all-to-all-start.2 = ((bf16[2,3,2,96,768]{4,2,1,0,3:T(2,128)(2,1)}), bf16[2,3,2,96,768]{4,2,1,0,3:T(2,128)(2,1)S(1)}, u32[]{:S(2)}, u32[]{:S(2)}) async-start(bf16[2,3,2,96,768]{4,2,1,0,3:T(2,128)(2,1)} %copy.104), calls=%async_computation.2 | async-start | bytes 3538944 | tf_op jit(solution)/shard_map/all_to_all | solution.py:128
  30.4 43.3 %copy-start.26 = (f32[2,8,96]{2,1,0:T(8,128)S(1)}, f32[2,8,96]{2,1,0:T(8,128)}, u32[]{:S(2)}) copy-start(f32[2,8,96]{2,1,0:T(8,128)} %param.13) | copy-start | bytes 18436
  30.4 43.3 %copy-start.27 = (f32[2,8,96]{2,1,0:T(8,128)S(1)}, f32[2,8,96]{2,1,0:T(8,128)}, u32[]{:S(2)}) copy-start(f32[2,8,96]{2,1,0:T(8,128)} %param.15) | copy-start | bytes 18436
  30.4 43.4 %copy-start.25 = (s32[8,96,3]{1,0,2:T(8,128)S(1)}, s32[8,96,3]{1,0,2:T(8,128)}, u32[]{:S(2)}) copy-start(s32[8,96,3]{1,0,2:T(8,128)} %param.10) | copy-start | bytes 27652
  30.4 45.4 %copy-start.6 = (bf16[2,8,96,96]{3,2,1,0:T(8,128)(2,1)S(1)}, bf16[2,8,96,96]{3,2,1,0:T(8,128)(2,1)}, u32[]{:S(2)}) copy-start(bf16[2,8,96,96]{3,2,1,0:T(8,128)(2,1)} %param.12) | copy-start | bytes 884740
  68.0 48.7 %all-to-all-start = ((bf16[2,3,2,96,768]{4,2,1,0,3:T(2,128)(2,1)}), bf16[2,3,2,96,768]{4,2,1,0,3:T(2,128)(2,1)}, u32[]{:S(2)}, u32[]{:S(2)}) async-start(bf16[2,3,2,96,768]{4,2,1,0,3:T(2,128)(2,1)} %copy.88), calls=%async_computation | async-start | bytes 3538944 | tf_op jit(solution)/shard_map/all_to_all | solution.py:104
  83.6 35.7 %copy-start.11 = (bf16[1,96,96,2]{2,1,3,0:T(8,128)(2,1)S(1)}, bf16[1,96,96,2]{2,1,3,0:T(8,128)(2,1)}, u32[]{:S(2)}) copy-start(bf16[1,96,96,2]{2,1,3,0:T(8,128)(2,1)} %copy-done.10) | copy-start | bytes 110596
  83.6 35.7 %copy-start.13 = (bf16[1,96,96,2]{2,1,3,0:T(8,128)(2,1)S(1)}, bf16[1,96,96,2]{2,1,3,0:T(8,128)(2,1)}, u32[]{:S(2)}) copy-start(bf16[1,96,96,2]{2,1,3,0:T(8,128)(2,1)} %copy-done.12) | copy-start | bytes 110596
  121.3 4.1 copy-start.4
  121.3 4.1 copy-start.5
  128.0 6.8 %copy-start = (bf16[2,2,96,3,8,96,1]{5,2,3,0,1,4,6:T(8,128)(2,1)}, bf16[2,2,96,3,8,96,1]{5,2,3,0,1,4,6:T(8,128)(2,1)S(1)}, u32[]{:S(2)}) copy-start(bf16[2,2,96,3,8,96,1]{5,2,3,0,1,4,6:T(8,128)(2,1)S(1)} %fusion.28) | copy-start | bytes 5308420
  147.3 4.7 copy-start.8
  147.3 4.7 copy-start.9
  157.2 48.3 %all-to-all-start.3 = ((bf16[2,96,2,3,768]{4,2,3,0,1:T(2,128)(2,1)}), bf16[2,96,2,3,768]{4,2,3,0,1:T(2,128)(2,1)}, u32[]{:S(2)}, u32[]{:S(2)}) async-start(bf16[2,96,2,3,768]{4,2,3,0,1:T(2,128)(2,1)} %copy.116), calls=%async_computation.3 | async-start | bytes 3538944 | tf_op jit(solution)/shard_map/all_to_all | solution.py:152
  205.5 282.4 %all-to-all-start.1 = ((bf16[2,96,2,3,768]{4,2,3,0,1:T(2,128)(2,1)}), bf16[2,96,2,3,768]{4,2,3,0,1:T(2,128)(2,1)}, u32[]{:S(2)}, u32[]{:S(2)}) async-start(bf16[2,96,2,3,768]{4,2,3,0,1:T(2,128)(2,1)} %copy.99), calls=%async_computation.1 | async-start | bytes 3538944 | tf_op jit(solution)/shard_map/all_to_all | solution.py:124
  210.5 266.9 %all-reduce.4.cloned.1.call-start = ((), (), s32[]{:S(2)}) async-start(), calls=%async_computation.4 | async-start | bytes 3145728 | tf_op jit(solution)/shard_map/psum | solution.py:145
  479.4 5.1 %copy-start.21 = (bf16[96,180]{0,1:T(8,128)(2,1)S(1)}, bf16[96,180]{0,1:T(8,128)(2,1)}, u32[]{:S(2)}) copy-start(bf16[96,180]{0,1:T(8,128)(2,1)} %copy-done.20) | copy-start | bytes 103684
  479.5 5.1 %copy-start.23 = (bf16[96,180]{0,1:T(8,128)(2,1)S(1)}, bf16[96,180]{0,1:T(8,128)(2,1)}, u32[]{:S(2)}) copy-start(bf16[96,180]{0,1:T(8,128)(2,1)} %copy-done.22) | copy-start | bytes 103684
  479.5 5.1 %copy-start.28 = (f32[3]{0:T(128)S(1)}, f32[3]{0:T(128)}, u32[]{:S(2)}) copy-start(f32[3]{0:T(128)} %get-tuple-element.30) | copy-start | bytes 40
  479.5 5.1 %copy-start.30 = (bf16[3]{0:T(256)(128)(2,1)S(1)}, bf16[3]{0:T(256)(128)(2,1)}, u32[]{:S(2)}) copy-start(bf16[3]{0:T(256)(128)(2,1)} %copy-done.29) | copy-start | bytes 22
  479.5 5.1 %copy-start.31 = (bf16[2,3,180,768]{3,0,2,1:T(2,128)(2,1)S(1)}, bf16[2,3,180,768]{3,0,2,1:T(2,128)(2,1)}, u32[]{:S(2)}) copy-start(bf16[2,3,180,768]{3,0,2,1:T(2,128)(2,1)} %param.9) | copy-start | bytes 4976644
  (14 other events, 35.2 us)
Sparse Core Ops, SparseCore 0:
  218.0 259.3 all-reduce.3
where the time goes:
time: 508 us; the launch traced here: 501 us
  waiting for transfers between devices  275 us (54%)
  blocking collectives  82.1 us (16%)
  local copies, waits for them, and re-layouts  58.2 us (11%)
  matrix products  31.3 us (6%)
  starting transfers between devices  26.3 us (5%)
  between operations  15.5 us (3%)
  other arithmetic  12.6 us (2%)
    psum x1, waiting for transfers between devices, on_device(): lax.psum((grad_one, bias_grad_one, grad_two, bias_grad_two), ('dp', 'spac...  176 us
    psum x1, blocking collectives, on_device(): lax.psum((grad_one, bias_grad_one, grad_two, bias_grad_two), ('dp', 'spac...  82.1 us
    all_to_all x1, waiting for transfers between devices, on_device(): lax.all_to_all(to_modes(gated, inverse_lon), 'space', split_axis=3, conca...  37.6 us
    all_to_all x1, waiting for transfers between devices, on_device(): lax.all_to_all(to_modes(masked, forward_lon), 'space', split_axis=3, conc...  33 us
    all_to_all x1, waiting for transfers between devices, on_device(): lax.all_to_all(d_lat, 'space', split_axis=1, concat_axis=3, tiled=True)  28.4 us
    all_to_all x1, starting transfers between devices, on_device(): lax.all_to_all(to_modes(gated, inverse_lon), 'space', split_axis=3, conca...  10.2 us
  transfers between devices with their start and end apart: 5, of which 4 were waited for; matrix products, arithmetic and copies ran while one was open for 10% of the time, Pallas kernels for 0%

commit v1 on v0

v1 whole, which is shorter than its diff:
```python
import numpy as np

import jax
import jax.numpy as jnp
from jax import lax
from jax.experimental import pallas as pl
from jax.experimental.pallas import tpu as pltpu
from jax.sharding import PartitionSpec as P

shrink = 0.25
gelu_scale = 0.7978845608028654
gelu_cubic = 0.044715

H = 96
W = 180
WP = 192
C = 768
HC = 384
NB = 8
BS = 96
KWP = 96
CHIPS = 16
IMAGES = 16
MESH = pl.DeviceIdType.MESH
f32 = jnp.float32
bf16 = jnp.bfloat16


def longitude_parts():
    wavenum = np.arange(KWP)[:, None]
    column = np.arange(W)[None, :]
    phase = np.float32(2.0 * np.pi / W) * (wavenum * column % W).astype(np.float32)
    scaling = (wavenum < W // 2 + 1).astype(np.float32) / np.sqrt(np.float32(W))
    double = np.where((wavenum == 0) | (2 * wavenum == W), 1.0, 2.0).astype(np.float32)
    cosine = np.cos(phase) * scaling
    sine = np.sin(phase) * scaling
    forward = np.stack([cosine, -sine])
    inverse = np.stack([double * cosine, -double * sine])
    return forward, inverse


def latitude_parts(sign):
    row = np.arange(H)[:, None]
    column = np.arange(H)[None, :]
    phase = np.float32(2.0 * np.pi / H) * (row * column % H).astype(np.float32)
    scaling = np.float32(1.0) / np.sqrt(np.float32(H))
    cosine = np.cos(phase) * scaling
    sine = np.float32(sign) * np.sin(phase) * scaling
    upper = np.stack([cosine, sine], -1)
    lower = np.stack([-sine, cosine], -1)
    return np.stack([upper, lower], 0)


def to_spectrum_table(part):
    out = np.zeros((3, 16, 4, 2, 2, 4, WP), np.float32)
    grouped = part.reshape(2, 16, 3, 2, W)
    for jj in range(4):
        out[:, :, jj, :, :, jj, :W] = grouped.transpose(2, 1, 0, 3, 4)
    return out.reshape(3, 256, 4 * WP)


def lat_tables():
    forward = latitude_parts(1.0)
    inverse = latitude_parts(-1.0)
    ahead = np.zeros((2, 2, 2, H, 16, 2, 6, 2, 2), np.float32)
    back = np.zeros((16, 2, 6, 2, 2, 2, 2, 2, H), np.float32)
    split = forward.reshape(2, H, 16, 6, 2)
    isplit = inverse.reshape(2, 16, 6, H, 2)
    for b in range(2):
        for kk in range(2):
            ahead[:, b, kk, :, :, b, :, :, kk] = split
            back[:, b, :, :, kk, :, b, kk, :] = isplit.transpose(1, 2, 0, 4, 3)
    return ahead.reshape(768, 768), back.reshape(768, 768)


def gelu_both(value):
    tangent = jnp.tanh(gelu_scale * (value + gelu_cubic * value * value * value))
    inner = gelu_scale * (1.0 + 3.0 * gelu_cubic * value * value)
    half = 0.5 * (1.0 + tangent)
    return value * half, half + 0.5 * value * (1.0 - tangent * tangent) * inner


def dot(left, right):
    return jnp.dot(left, right, preferred_element_type=f32)


def kernel(
    x_in, c_in, kept_in, w_one, w_two, b_in, ft_in, tt_in, lf_in, li_in,
    out_x, out_c, gw_one, gb_one, gw_two, gb_two,
    xs, fts, tts, lfs, lis, wraw, wd, keeps,
    send, got, facc, spec, hid, slope, kt, tmp, fil, dtwo, gacc, bacc,
    gp, gy, s_one, gx, s_two, gz, fx, fy, fc,
    load_sem, xin_send, xin_recv, ssem, rsem, oloc, osend, orecv, gsend, grecv,
):
    me = lax.axis_index("space")
    dp = lax.axis_index("dp")
    core = lax.rem(me, 2)
    other = 1 - core
    m = me // 2
    y = m // 4
    z = lax.rem(m, 4)
    zh = dp // 4
    x = lax.rem(dp, 4)
    buddy = (dp, 2 * m + other)
    mine = pl.ds(pl.multiple_of(core * HC, 128), HC)
    theirs = pl.ds(pl.multiple_of(other * HC, 128), HC)

    def load(src, dst, at):
        return pltpu.make_async_copy(src, dst, load_sem.at[at])

    own = []
    for v, ref in ((0, x_in), (1, c_in)):
        for b in range(2):
            own.append(load(ref.at[b, :, :, mine], xs.at[v, pl.ds(b * 6 + 3 * core, 3)], 2 * v + b))
    kept_own = load(kept_in.at[:, :, mine], keeps.at[pl.ds(3 * core, 3)], 4)
    tables = [
        load(ft_in.at[0], fts.at[0], 5),
        load(ft_in.at[1], fts.at[1], 6),
        load(lf_in, lfs, 7),
        load(w_one, wraw.at[0], 8),
        load(w_two, wraw.at[1], 11),
        load(li_in, lis, 9),
        load(tt_in, tts, 10),
    ]
    for copy in own[:2] + tables[:1] + own[2:] + tables[1:2] + [kept_own] + tables[2:]:
        copy.start()

    barrier = pltpu.get_barrier_semaphore()

    def greet_group(i, carry):
        peer = 2 * lax.rem(m + i, CHIPS) + core
        pl.semaphore_signal(barrier, inc=1, device_id=(dp, peer), device_id_type=MESH)
        return carry

    lax.fori_loop(1, CHIPS, greet_group, 0)
    pl.semaphore_signal(barrier, inc=1, device_id=buddy, device_id_type=MESH)
    for i in range(1, 4):
        pl.semaphore_signal(
            barrier, inc=1, device_id=(zh * 4 + lax.rem(x + i, 4), me), device_id_type=MESH
        )
    for i in range(4):
        far = (lax.rem(dp + 4, 8), 2 * (y * 4 + lax.rem(z + i, 4)) + core)
        pl.semaphore_signal(barrier, inc=1, device_id=far, device_id_type=MESH)
    pl.semaphore_wait(barrier, 15 + 1 + 3 + 4)

    swaps = []
    for v, ref in ((0, x_in), (1, c_in)):
        for b in range(2):
            swaps.append(
                pltpu.make_async_remote_copy(
                    src_ref=ref.at[b, :, :, theirs],
                    dst_ref=xs.at[v, pl.ds(b * 6 + 3 * core, 3)],
                    send_sem=xin_send.at[2 * v + b],
                    recv_sem=xin_recv.at[2 * v + b],
                    device_id=buddy,
                    device_id_type=MESH,
                )
            )
    swaps.append(
        pltpu.make_async_remote_copy(
            src_ref=kept_in.at[:, :, theirs],
            dst_ref=keeps.at[pl.ds(3 * core, 3)],
            send_sem=xin_send.at[4],
            recv_sem=xin_recv.at[4],
            device_id=buddy,
            device_id_type=MESH,
        )
    )
    for copy in swaps:
        copy.start()

    def send_chunk(phase, a):
        def one(i, carry):
            peer = lax.rem(m + i, CHIPS)
            pltpu.make_async_remote_copy(
                src_ref=send.at[phase, a, peer],
                dst_ref=got.at[phase, a, m],
                send_sem=ssem.at[phase, a],
                recv_sem=rsem.at[phase, a],
                device_id=(dp, 2 * peer + core),
                device_id_type=MESH,
            ).start()
            return carry

        lax.fori_loop(1, CHIPS, one, 0)

    def wait_chunk(phase, a, sem):
        whole = got.at[phase, a, pl.ds(0, 15)]
        pltpu.make_async_copy(whole, whole, sem.at[phase, a]).wait()

    def to_spectrum(v):
        def one(a, carry):
            for t in range(3):
                field = xs[v, 4 * t : 4 * t + 4].reshape(768, HC)
                result = dot(fts[v, a], field).astype(bf16).reshape(16, 16, HC)
                send[v, a, :, 16 * t : 16 * t + 16, :] = result
            send_chunk(v, a)
            got[v, a, m] = send[v, a, m]
            return carry

        lax.fori_loop(0, 3, one, 0)

    for v in range(2):
        for b in range(2):
            own[2 * v + b].wait()
            swaps[2 * v + b].wait()
        tables[v].wait()
        to_spectrum(v)

    gacc[...] = jnp.zeros_like(gacc)
    bacc[...] = jnp.zeros_like(bacc)
    for copy in [kept_own, swaps[4]] + tables[2:]:
        copy.wait()
    lane = lax.broadcasted_iota(jnp.int32, (BS, HC), 1)
    line = lax.broadcasted_iota(jnp.int32, (BS, HC), 0)
    for mat in range(2):
        for n in range(4):
            select = jnp.where(lane == line + BS * n, 1.0, 0.0).astype(bf16)
            real = dot(wraw[mat, 0, 4 * core + n], select)
            imag = dot(wraw[mat, 1, 4 * core + n], select)
            up, down = BS * n, HC + BS * n
            wd[mat, up : up + BS, :HC] = real.astype(bf16)
            wd[mat, up : up + BS, HC:] = imag.astype(bf16)
            wd[mat, down : down + BS, :HC] = (-imag).astype(bf16)
            wd[mat, down : down + BS, HC:] = real.astype(bf16)

    def spectral(phase, a, half):
        field = got[phase, a].reshape(768, HC)
        return dot(lfs[half * HC : half * HC + HC, :], field)

    def unspectral(phase, a):
        for t in range(2):
            result = dot(lis[t * HC : t * HC + HC, :], fil[...]).astype(bf16)
            send[phase, a, 8 * t : 8 * t + 8] = result.reshape(8, 48, HC)
        got[phase, a, m] = send[phase, a, m]

    def product(left, mat):
        for n in range(3):
            tmp[:, 256 * n : 256 * n + 256] = dot(left, wd[mat, :, 256 * n : 256 * n + 256])

    def product_turned(left, mat):
        for n in range(3):
            tmp[:, 256 * n : 256 * n + 256] = lax.dot_general(
                left,
                wd[mat, 256 * n : 256 * n + 256, :],
                (((1,), (1,)), ((), ())),
                preferred_element_type=f32,
            )

    def rows_of(step):
        return pl.ds(pl.multiple_of(step * 32, 32), 32)

    def kept_rows(a, step):
        kk = lax.rem(step // 3, 2)
        q = pl.multiple_of(lax.rem(step, 3) * 32, 32)
        return keeps[2 * a + kk, pl.ds(q, 32), :].astype(f32)

    def forward(a, carry):
        wait_chunk(0, a, rsem)
        for p in range(2):
            spec[a, :, p * HC : p * HC + HC] = spectral(0, a, p).astype(bf16)
        product(spec[a], 0)

        def gelu_rows(step, carry):
            rows = rows_of(step)
            for p in range(2):
                part = slice(p * HC, p * HC + HC)
                value, tilt = gelu_both(tmp[rows, part] + b_in[0, core, p])
                hid[a, rows, part] = value.astype(bf16)
                slope[a, rows, part] = tilt
            return carry

        lax.fori_loop(0, 12, gelu_rows, 0)
        product(hid[a], 1)

        def shrink_rows(step, carry):
            rows = rows_of(step)
            kept = kept_rows(a, step)
            for p in range(2):
                part = slice(p * HC, p * HC + HC)
                value = tmp[rows, part] + b_in[1, core, p]
                tangent = jnp.tanh(value * (1.0 / shrink))
                filtered = (value - shrink * tangent) * kept
                fil[pl.ds(pl.multiple_of(p * HC + step * 32, 32), 32), :] = filtered.astype(bf16)
                kt[a, rows, part] = kept * (tangent * tangent)
            return carry

        lax.fori_loop(0, 12, shrink_rows, 0)
        unspectral(2, a)
        return carry

    lax.fori_loop(0, 3, forward, 0)
    send_chunk(2, 0)

    def add_grad(mat, left, right):
        for n in range(3):
            part = slice(256 * n, 256 * n + 256)
            gacc[mat, :, part] += lax.dot_general(
                left, right[:, part], (((0,), (0,)), ((), ())), preferred_element_type=f32
            )

    def backward(a, carry):
        wait_chunk(1, a, rsem)
        for p in range(2):
            tmp[:, p * HC : p * HC + HC] = spectral(1, a, p)

        def scaled_rows(mat, scale):
            def one(step, carry):
                rows = rows_of(step)
                for p in range(2):
                    part = slice(p * HC, p * HC + HC)
                    value = (tmp[rows, part] * scale[a, rows, part]).astype(bf16)
                    dtwo[rows, part] = value
                    bacc[mat, :, part] += value.astype(f32).reshape(4, 8, HC).sum(0)
                return carry

            lax.fori_loop(0, 12, one, 0)

        scaled_rows(1, kt)
        add_grad(1, hid[a], dtwo[...])
        product_turned(dtwo[...], 1)
        scaled_rows(0, slope)
        add_grad(0, spec[a], dtwo[...])
        product_turned(dtwo[...], 0)
        for p in range(2):
            fil[p * HC : p * HC + HC, :] = tmp[:, p * HC : p * HC + HC].astype(bf16)
        unspectral(3, a)
        return carry

    lax.fori_loop(0, 3, backward, 0)

    for mat in range(2):
        for n in range(4):
            start = BS * n // 128 * 128
            shift = BS * n - start
            window = 256 if shift + BS > 128 else 128
            up = slice(BS * n, BS * n + BS)
            down = slice(HC + BS * n, HC + BS * n + BS)
            left = slice(start, start + window)
            right = slice(HC + start, HC + start + window)

            def align(value):
                if shift:
                    value = pltpu.roll(value, window - shift, 1)
                return value[:, :128]

            gp[n, 2 * mat, :BS, :] = align(gacc[mat, up, left] + gacc[mat, down, right])
            gp[n, 2 * mat + 1, :BS, :] = align(gacc[mat, up, right] - gacc[mat, down, left])
            gp[n, 2 * mat, BS:, :] = align(bacc[mat, :, left])
            gp[n, 2 * mat + 1, BS:, :] = align(bacc[mat, :, right])

    def gather(count, source, target, device, at):
        def copy(i):
            return pltpu.make_async_remote_copy(
                src_ref=source(i),
                dst_ref=target,
                send_sem=gsend.at[at],
                recv_sem=grecv.at[at],
                device_id=device(i),
                device_id_type=MESH,
            )

        for i in range(count):
            copy(i).start()

    def settle(part, at):
        pltpu.make_async_copy(part, part, grecv.at[at]).wait()

    def row_peer(i):
        return lax.rem(y + 1 + i, 4)

    def x_peer(i):
        return lax.rem(x + 1 + i, 4)

    def row_device(i):
        return (dp, 2 * (row_peer(i) * 4 + z) + core)

    def x_device(i):
        return (zh * 4 + x_peer(i), me)

    def z_device(i):
        if i < 3:
            return (dp, 2 * (y * 4 + lax.rem(z + 1 + i, 4)) + core)
        return (lax.rem(dp + 4, 8), 2 * (y * 4 + lax.rem(z + i - 3, 4)) + core)

    gather(3, lambda i: gp.at[row_peer(i)], gy.at[y], row_device, 0)
    send_chunk(2, 1)
    gy[y] = gp[y]
    settle(gy.at[pl.ds(0, 3)], 0)
    s_one[...] = (gy[0] + gy[1]) + (gy[2] + gy[3])
    gather(3, lambda i: s_one.at[x_peer(i)], gx.at[x], x_device, 1)
    send_chunk(2, 2)
    gx[x] = s_one[x]
    settle(gx.at[pl.ds(0, 3)], 1)
    s_two[...] = (gx[0] + gx[1]) + (gx[2] + gx[3])
    gather(7, lambda i: s_two, gz.at[zh * 4 + z], z_device, 2)
    send_chunk(3, 0)
    gz[zh * 4 + z] = s_two[...]
    settle(gz.at[pl.ds(0, 7)], 2)
    total = gz[0]
    for i in range(1, 8):
        total = total + gz[i]
    fx[x] = total * (1.0 / (IMAGES * H))
    gather(3, lambda i: fx.at[x], fx.at[x], x_device, 3)
    send_chunk(3, 1)
    settle(fx.at[pl.ds(0, 3)], 3)
    fy[y] = fx[...]
    gather(3, lambda i: fy.at[y], fy.at[y], row_device, 4)
    send_chunk(3, 2)
    settle(fy.at[pl.ds(0, 3)], 4)
    gather(1, lambda i: fy, fc, lambda i: buddy, 5)

    def leave(v):
        def part(a, carry):
            wait_chunk(2 + v, a, rsem)

            def one(t, carry):
                piece = got[2 + v, a, :, pl.ds(pl.multiple_of(16 * t, 16), 16), :]
                piece = piece.reshape(256, HC)
                for j in range(4):
                    rows = pl.ds(j * WP, WP)
                    facc[t, rows, :] += dot(tts[1 - v, a, j * WP : j * WP + WP, :], piece)
                return carry

            lax.fori_loop(0, 3, one, 0)
            return carry

        def begin(t, carry):
            facc[t] = xs[v, pl.ds(4 * t, 4)].reshape(768, HC).astype(f32)
            return carry

        def finish(t, carry):
            xs[v, pl.ds(4 * t, 4)] = facc[t].astype(bf16).reshape(4, WP, HC)
            return carry

        lax.fori_loop(0, 3, begin, 0)
        lax.fori_loop(0, 3, part, 0)
        lax.fori_loop(0, 3, finish, 0)
        ref = (out_x, out_c)[v]
        copies = []
        for b in range(2):
            copies.append(
                pltpu.make_async_remote_copy(
                    src_ref=xs.at[v, pl.ds(b * 6 + 3 * other, 3)],
                    dst_ref=ref.at[b, :, :, mine],
                    send_sem=osend.at[2 * v + b],
                    recv_sem=orecv.at[2 * v + b],
                    device_id=buddy,
                    device_id_type=MESH,
                )
            )
            copies[-1].start()
        for b in range(2):
            copies.append(
                pltpu.make_async_copy(
                    xs.at[v, pl.ds(b * 6 + 3 * core, 3)], ref.at[b, :, :, mine], oloc.at[2 * v + b]
                )
            )
            copies[-1].start()
        return copies

    leaving = leave(0)

    settle(fc, 5)
    for half, held in ((core, fy), (other, fc)):

        def one(n, carry):
            for mat, (weight, bias) in enumerate(((gw_one, gb_one), (gw_two, gb_two))):
                for p in range(2):
                    weight[p, 4 * half + n] = held[n, 2 * mat + p, :BS, :BS]
                    bias[p, 4 * half + n] = held[n, 2 * mat + p, BS:, :BS].sum(0, keepdims=True)
            return carry

        lax.fori_loop(0, 4, one, 0)

    leaving += leave(1)
    for copy in leaving:
        copy.wait()

    def sent(i, carry):
        wait_chunk(i // 3, lax.rem(i, 3), ssem)
        return carry

    lax.fori_loop(0, 12, sent, 0)
    for at, part in (
        (0, gy.at[pl.ds(0, 3)]),
        (1, gx.at[pl.ds(0, 3)]),
        (2, gz.at[pl.ds(0, 7)]),
        (3, fx.at[pl.ds(0, 3)]),
        (4, fy.at[pl.ds(0, 3)]),
        (5, fc),
    ):
        pltpu.make_async_copy(part, part, gsend.at[at]).wait()


def mix(x_pad, c_pad, kept, w_one, w_two, bias):
    forward_lon, inverse_lon = longitude_parts()
    ahead = np.stack([to_spectrum_table(forward_lon), to_spectrum_table(inverse_lon)])
    lf, li = lat_tables()
    as_bf16 = lambda table: jnp.asarray(table.astype(jnp.bfloat16))
    tables = (as_bf16(ahead), as_bf16(ahead.transpose(0, 1, 3, 2)), as_bf16(lf), as_bf16(li))
    anywhere = pl.BlockSpec(memory_space=pl.ANY)
    vmem = pl.BlockSpec(memory_space=pltpu.VMEM)
    dma = pltpu.SemaphoreType.DMA
    return pl.pallas_call(
        kernel,
        out_shape=(
            jax.ShapeDtypeStruct(x_pad.shape, bf16),
            jax.ShapeDtypeStruct(c_pad.shape, bf16),
            jax.ShapeDtypeStruct((2, NB, BS, BS), f32),
            jax.ShapeDtypeStruct((2, NB, 1, BS), f32),
            jax.ShapeDtypeStruct((2, NB, BS, BS), f32),
            jax.ShapeDtypeStruct((2, NB, 1, BS), f32),
        ),
        in_specs=[anywhere] * 5 + [vmem] + [anywhere] * 4,
        out_specs=(anywhere, anywhere, vmem, vmem, vmem, vmem),
        scratch_shapes=[
            pltpu.VMEM((2, 12, WP, HC), bf16),
            pltpu.VMEM((2, 3, 256, 768), bf16),
            pltpu.VMEM((2, 3, 768, 256), bf16),
            pltpu.VMEM((768, 768), bf16),
            pltpu.VMEM((768, 768), bf16),
            pltpu.VMEM((2, 2, NB, BS, BS), bf16),
            pltpu.VMEM((2, 768, 768), bf16),
            pltpu.VMEM((6, H, HC), bf16),
            pltpu.VMEM((4, 3, CHIPS, 48, HC), bf16),
            pltpu.VMEM((4, 3, CHIPS, 48, HC), bf16),
            pltpu.VMEM((3, 768, HC), f32),
            pltpu.VMEM((3, HC, 768), bf16),
            pltpu.VMEM((3, HC, 768), bf16),
            pltpu.VMEM((3, HC, 768), f32),
            pltpu.VMEM((3, HC, 768), f32),
            pltpu.VMEM((HC, 768), f32),
            pltpu.VMEM((768, HC), bf16),
            pltpu.VMEM((HC, 768), bf16),
            pltpu.VMEM((2, 768, 768), f32),
            pltpu.VMEM((2, 8, 768), f32),
            pltpu.VMEM((4, 4, 104, 128), f32),
            pltpu.VMEM((4, 4, 104, 128), f32),
            pltpu.VMEM((4, 104, 128), f32),
            pltpu.VMEM((4, 104, 128), f32),
            pltpu.VMEM((104, 128), f32),
            pltpu.VMEM((8, 104, 128), f32),
            pltpu.VMEM((4, 104, 128), f32),
            pltpu.VMEM((4, 4, 104, 128), f32),
            pltpu.VMEM((4, 4, 104, 128), f32),
            dma((12,)),
            dma((5,)),
            dma((5,)),
            dma((4, 3)),
            dma((4, 3)),
            dma((4,)),
            dma((4,)),
            dma((4,)),
            dma((6,)),
            dma((6,)),
        ],
        compiler_params=pltpu.CompilerParams(
            collective_id=0, has_side_effects=True, vmem_limit_bytes=61 * 2**20
        ),
    )(x_pad, c_pad, kept, w_one, w_two, bias, *tables)


def on_device(inputs, cotangent, kept_modes, pad_rows, weight_one, bias_one, weight_two, bias_two):
    rows = inputs.shape[1]
    local_modes = kept_modes.shape[2]
    place = lax.axis_index("space")
    row_ids = place * rows + jnp.arange(rows, dtype=jnp.int32)
    valid = (row_ids < H - pad_rows[0]).astype(bf16)[None, :, None, None]
    mode_ids = place * local_modes + jnp.arange(local_modes, dtype=jnp.int32)
    kept = kept_modes * (mode_ids < W // 2 + 1).astype(jnp.int32)[None, None, :]
    kept = jnp.transpose(kept, (2, 1, 0)).astype(bf16)
    kept = jnp.broadcast_to(kept[..., None], (local_modes, H, NB, BS)).reshape(local_modes, H, C)
    margin = ((0, 0), (0, 0), (0, WP - W), (0, 0))
    x_pad = jnp.pad(inputs * valid, margin)
    c_pad = jnp.pad(cotangent * valid, margin)
    bias = jnp.stack([bias_one.reshape(2, 2, HC), bias_two.reshape(2, 2, HC)])
    bias = jnp.transpose(bias, (0, 2, 1, 3))[:, :, :, None, :]
    out_x, out_c, gw_one, gb_one, gw_two, gb_two = mix(
        x_pad, c_pad, kept, weight_one, weight_two, bias
    )
    return (
        out_x[:, :, :W] * valid,
        out_c[:, :, :W] * valid,
        gw_one,
        gb_one[:, :, 0],
        gw_two,
        gb_two[:, :, 0],
    )


def solution(mesh):
    placed = (
        P("dp", "space", None, None),
        P("dp", "space", None, None),
        P(None, None, "space"),
        P(),
        P(),
        P(),
        P(),
        P(),
    )
    return jax.shard_map(
        on_device,
        mesh=mesh,
        in_specs=placed,
        out_specs=(P("dp", "space", None, None), P("dp", "space", None, None), P(), P(), P(), P()),
        check_vma=False,
    )
```

time: 508 us -> 207 us (0.41); the launches traced: 501 us -> 207 us
  waiting for transfers between devices: 275 us -> 0 us
  Pallas kernels: 0 us -> 186 us
  blocking collectives: 82.1 us -> 0 us
  local copies, waits for them, and re-layouts: 58.2 us -> 14.5 us
  matrix products: 31.3 us -> 0 us
  starting transfers between devices: 26.3 us -> 0 us
  between operations: 15.5 us -> 1.46 us
  other arithmetic: 12.6 us -> 4.96 us
    pallas_call x0 -> x1, Pallas kernels: none -> 186 us  [mix(): pl.pallas_call(kernel, out_shape=(jax.ShapeDtypeStruct(x_pad.shape, bf16)...]
    psum x1 -> x0, waiting for transfers between devices: 176 us -> none  [on_device(): lax.psum((grad_one, bias_grad_one, grad_two, bias_grad_two), ('dp', 'spac...]
    all_to_all x4 -> x0, waiting for transfers between devices: 98.9 us -> none  [the longest x1 37.6 us: on_device(): lax.all_to_all(to_modes(gated, inverse_lon), 'space', split_axis=3, conca...]
    psum x1 -> x0, blocking collectives: 82.1 us -> none  [on_device(): lax.psum((grad_one, bias_grad_one, grad_two, bias_grad_two), ('dp', 'spac...]
    reshape x8 -> x1, local copies, waits for them, and re-layouts: 32.5 us -> 1.22 us  [on_device(): jnp.broadcast_to(kept[..., None], (local_modes, H, NB, BS))]
    dot_general x14 -> x0, matrix products: 31.3 us -> none  [the longest x1 6.78 us: on_device(): jnp.einsum('brhknc,nrcpd->bphknd', hidden, big_two, preferred_element_typ...]
    all_to_all x4 -> x0, starting transfers between devices: 26.3 us -> none  [the longest x1 10.2 us: on_device(): lax.all_to_all(to_modes(gated, inverse_lon), 'space', split_axis=3, conca...]
    all_to_all x4 -> x0, local copies, waits for them, and re-layouts: 9.71 us -> none  [the longest x1 2.97 us: on_device(): lax.all_to_all(back_lat, 'space', split_axis=1, concat_axis=3, tiled=True)]
  transfers between devices with their start and end apart: 5 -> 0, of which waited for: 4 -> 0; matrix products, arithmetic and copies ran while one was open for 10% -> 0% of each run, Pallas kernels for 0% -> 0%
where the time goes in v1:
time: 207 us
  Pallas kernels  186 us (90%)
  local copies, waits for them, and re-layouts  14.5 us (7%)
  other arithmetic  4.96 us (2%)
    pallas_call x1, Pallas kernels, mix(): pl.pallas_call(kernel, out_shape=(jax.ShapeDtypeStruct(x_pad.shape, bf16)...  186 us
    unnamed x16, local copies, waits for them, and re-layouts  7.87 us

profile of v1, /device:TPU:1, one launch (start us, length us, event | category | flops | bytes accessed | tf_op | source)
XLA Modules:
  0.0 206.6 jit_solution(5274933397415990168)
XLA Ops:
  0.6 0.0 copy-start
  1.4 0.8 fusion
  2.2 0.8 stack_reshape.6
  3.0 0.8 stack_reshape.7
  3.8 0.6 broadcast_in_dim.5.b_in
  4.4 0.1 copy.25
  4.5 0.4 broadcast_in_dim.4
  4.9 1.2 reshape.30.kept_in
  6.1 0.0 copy-done
  6.2 1.9 copy_multiply_fusion
  8.1 1.3 pad.8.c_in
  9.4 1.4 pad.7.x_in
  10.7 185.7 %shard_map.163 = (bf16[2,3,192,768]{3,2,1,0:T(8,128)(2,1)}, bf16[2,3,192,768]{3,2,1,0:T(8,128)(2,1)}, f32[2,8,96,96]{3,2,1,0:T(8,128)}, f32[2,8,1,96]{3,2,1,0:T(...) custom-call(bf16[2,3,192,768]{3,2,1,0:T(8,128)(2,1)} %pad.7.x_in, bf16[2,3,192,768]{3,2,1,0:T(8,128)(2,1)} %pad.8.c_in, ...), custom_call_target="tpu_custom_call" | custom-call | tf_op jit(solution)/shard_map/pallas_call | solution.py:505
  196.4 2.3 %slice_multiply_fusion = (bf16[2,3,180,768]{3,2,1,0:T(8,128)(2,1)S(1)}, bf16[2,3,180,768]{3,2,1,0:T(8,128)(2,1)S(1)}) fusion(bf16[2,3,192,768]{3,2,1,0:T(8,128)(2,1)} %get-tuple-element.13, bf16[3]{0:T(256)(128)(2,1)S(1)} %get-tuple-element.35, bf16[2,3,192,768]{3,2,1,0:T(8,128)(2,1)} %get-tuple-element.12), kind=kLoop, calls=%fused_computation.2 | loop fusion | flops 1658880 | bytes 6635526 | tf_op jit(solution)/shard_map/mul | solution.py:584
  198.7 2.5 %copy.29 = bf16[2,3,180,768]{3,0,2,1:T(2,128)(2,1)} copy(bf16[2,3,180,768]{3,2,1,0:T(8,128)(2,1)S(1)} %get-tuple-element.30) | data formatting | bytes 3317760
  201.2 2.4 %copy.28 = bf16[2,3,180,768]{3,0,2,1:T(2,128)(2,1)} copy(bf16[2,3,180,768]{3,2,1,0:T(8,128)(2,1)S(1)} %get-tuple-element.31) | data formatting | bytes 3317760
  203.6 0.0 copy-done.2
  203.6 0.9 copy.37
  204.5 0.0 copy-done.4
  204.5 0.6 copy.38
  205.1 0.0 copy-done.1
  205.1 0.9 copy.39
  206.0 0.0 copy-done.3
  206.0 0.6 copy.40
  (8 shorter events, 0.0 us)
Async XLA Ops:
  0.6 5.5 %copy-start = (bf16[2,3,180,768]{3,0,2,1:T(2,128)(2,1)S(1)}, bf16[2,3,180,768]{3,0,2,1:T(2,128)(2,1)}, u32[]{:S(2)}) copy-start(bf16[2,3,180,768]{3,0,2,1:T(2,128)(2,1)} %param.13) | copy-start | bytes 4976644
  201.2 2.5 %copy-start.2 = (f32[2,8,96,96]{3,2,1,0:T(8,128)S(1)}, f32[2,8,96,96]{3,2,1,0:T(8,128)}, u32[]{:S(2)}) copy-start(f32[2,8,96,96]{3,2,1,0:T(8,128)} %get-tuple-element.44) | copy-start | bytes 1769476
  201.2 3.3 %copy-start.4 = (f32[2,8,1,96]{3,2,1,0:T(1,128)S(1)}, f32[2,8,1,96]{3,2,1,0:T(1,128)}, u32[]{:S(2)}) copy-start(f32[2,8,1,96]{3,2,1,0:T(1,128)} %get-tuple-element.15) | copy-start | bytes 18436
  201.2 3.9 %copy-start.1 = (f32[2,8,96,96]{3,2,1,0:T(8,128)S(1)}, f32[2,8,96,96]{3,2,1,0:T(8,128)}, u32[]{:S(2)}) copy-start(f32[2,8,96,96]{3,2,1,0:T(8,128)} %get-tuple-element.46) | copy-start | bytes 1769476
  203.6 2.4 %copy-start.3 = (f32[2,8,1,96]{3,2,1,0:T(1,128)S(1)}, f32[2,8,1,96]{3,2,1,0:T(1,128)}, u32[]{:S(2)}) copy-start(f32[2,8,1,96]{3,2,1,0:T(1,128)} %get-tuple-element.17) | copy-start | bytes 18436

commit v2 on v1

v2 whole, which is shorter than its diff:
```python
import numpy as np

import jax
import jax.numpy as jnp
from jax import lax
from jax.experimental import pallas as pl
from jax.experimental.pallas import tpu as pltpu
from jax.sharding import PartitionSpec as P

shrink = 0.25
gelu_scale = 0.7978845608028654
gelu_cubic = 0.044715

H = 96
W = 180
WIDE = 768
C = 768
HC = 384
NB = 8
BS = 96
KWP = 96
CHIPS = 16
IMAGES = 16
MESH = pl.DeviceIdType.MESH
f32 = jnp.float32
bf16 = jnp.bfloat16


def longitude_parts():
    wavenum = np.arange(KWP)[:, None]
    column = np.arange(W)[None, :]
    phase = np.float32(2.0 * np.pi / W) * (wavenum * column % W).astype(np.float32)
    scaling = (wavenum < W // 2 + 1).astype(np.float32) / np.sqrt(np.float32(W))
    double = np.where((wavenum == 0) | (2 * wavenum == W), 1.0, 2.0).astype(np.float32)
    cosine = np.cos(phase) * scaling
    sine = np.sin(phase) * scaling
    forward = np.stack([cosine, -sine])
    inverse = np.stack([double * cosine, -double * sine])
    return forward, inverse


def latitude_parts(sign):
    row = np.arange(H)[:, None]
    column = np.arange(H)[None, :]
    phase = np.float32(2.0 * np.pi / H) * (row * column % H).astype(np.float32)
    scaling = np.float32(1.0) / np.sqrt(np.float32(H))
    cosine = np.cos(phase) * scaling
    sine = np.float32(sign) * np.sin(phase) * scaling
    upper = np.stack([cosine, sine], -1)
    lower = np.stack([-sine, cosine], -1)
    return np.stack([upper, lower], 0)


def to_spectrum_table(part):
    out = np.zeros((3, 16, 2, 2, 2, 2, 2, W, 2), np.float32)
    grouped = part.reshape(2, 16, 3, 2, W).transpose(2, 1, 0, 3, 4)
    for jj in range(2):
        for b in range(2):
            out[:, :, jj, b, :, :, jj, :, b] = grouped
    out = out.reshape(3, 256, 4 * W)
    return np.pad(out, ((0, 0), (0, 0), (0, WIDE - 4 * W)))


def lat_tables():
    forward = latitude_parts(1.0)
    inverse = latitude_parts(-1.0)
    ahead = np.zeros((2, 2, 2, H, 16, 6, 2, 2, 2), np.float32)
    back = np.zeros((16, 6, 2, 2, 2, 2, 2, 2, H), np.float32)
    split = forward.reshape(2, H, 16, 6, 2)
    isplit = inverse.reshape(2, 16, 6, H, 2)
    for b in range(2):
        for kk in range(2):
            ahead[:, b, kk, :, :, :, b, :, kk] = split
            back[:, :, b, :, kk, :, b, kk, :] = isplit.transpose(1, 2, 0, 4, 3)
    return ahead.reshape(768, 768), back.reshape(768, 768)


def gelu_both(value):
    tangent = jnp.tanh(gelu_scale * (value + gelu_cubic * value * value * value))
    inner = gelu_scale * (1.0 + 3.0 * gelu_cubic * value * value)
    half = 0.5 * (1.0 + tangent)
    return value * half, half + 0.5 * value * (1.0 - tangent * tangent) * inner


def dot(left, right):
    return jnp.dot(left, right, preferred_element_type=f32)


def kernel(
    x_in, c_in, kept_in, pad_in, w_one, w_two, b_one, b_two, ft_in, tt_in, lf_in, li_in,
    out_x, out_c, gw_one, gb_one, gw_two, gb_two,
    xs, fts, tts, lfs, lis, wraw, wd, kraw, keeps, brow,
    send, got, facc, spec, hid, slope, kt, tmp, fil, dtwo, gacc, bacc,
    gp, gr, s_two, gz, s_three, fin, fy, fc,
    load_sem, xown, xin_send, xin_recv, ssem, rsem, oloc, osend, orecv, gsend, grecv,
):
    me = lax.axis_index("space")
    dp = lax.axis_index("dp")
    core = lax.rem(me, 2)
    other = 1 - core
    m = me // 2
    y = m // 4
    z = lax.rem(m, 4)
    zh = dp // 4
    x = lax.rem(dp, 4)
    depth = zh * 4 + z
    buddy = (dp, 2 * m + other)

    def tile(which, l):
        return pl.ds(pl.multiple_of(which * HC + l * 128, 128), 128)

    def row_slot(v, j6, l):
        return xs.at[v, j6 // 2, l, pl.ds(lax.rem(j6, 2) * W, W)]

    def row_slots(v, j6):
        return xs.at[v, j6 // 2, :, pl.ds(lax.rem(j6, 2) * W, W)]

    def load(src, dst, at):
        return pltpu.make_async_copy(src, dst, load_sem.at[at])

    def start_own(v, ref):
        for j in range(3):
            for l in range(3):
                pltpu.make_async_copy(
                    ref.at[j, :, :, tile(core, l)], row_slot(v, 3 * core + j, l), xown.at[v, j]
                ).start()

    kept_own = load(kept_in, kraw.at[pl.ds(3 * core, 3)], 0)
    tables = [
        load(ft_in.at[0], fts.at[0], 1),
        load(ft_in.at[1], fts.at[1], 2),
        load(lf_in, lfs, 3),
        load(w_one, wraw.at[0], 4),
        load(w_two, wraw.at[1], 5),
        load(li_in, lis, 6),
        load(tt_in, tts, 7),
    ]
    start_own(0, x_in)
    tables[0].start()
    start_own(1, c_in)
    for copy in tables[1:2] + [kept_own] + tables[2:]:
        copy.start()

    barrier = pltpu.get_barrier_semaphore()

    def greet(device):
        pl.semaphore_signal(barrier, inc=1, device_id=device, device_id_type=MESH)

    def greet_group(i, carry):
        greet((dp, 2 * lax.rem(m + i, CHIPS) + core))
        return carry

    def plane_device(i):
        row = lax.rem(y + i // 4, 4)
        return (zh * 4 + lax.rem(x + lax.rem(i, 4), 4), 2 * (row * 4 + z) + core)

    def greet_plane(i, carry):
        greet(plane_device(4 * (i // 3) + lax.rem(i, 3) + 1))
        return carry

    lax.fori_loop(1, CHIPS, greet_group, 0)
    greet(buddy)
    lax.fori_loop(0, 12, greet_plane, 0)
    for i in range(4):
        greet((lax.rem(dp + 4, 8), 2 * (y * 4 + lax.rem(z + i, 4)) + core))
    pl.semaphore_wait(barrier, 15 + 1 + 12 + 4)

    def swap(v, ref):
        for j in range(3):
            for l in range(3):
                pltpu.make_async_remote_copy(
                    src_ref=ref.at[j, :, :, tile(other, l)],
                    dst_ref=row_slot(v, 3 * core + j, l),
                    send_sem=xin_send.at[v, j],
                    recv_sem=xin_recv.at[v, j],
                    device_id=buddy,
                    device_id_type=MESH,
                ).start()

    kept_swap = pltpu.make_async_remote_copy(
        src_ref=kept_in,
        dst_ref=kraw.at[pl.ds(3 * core, 3)],
        send_sem=xin_send.at[2, 0],
        recv_sem=xin_recv.at[2, 0],
        device_id=buddy,
        device_id_type=MESH,
    )
    swap(0, x_in)
    swap(1, c_in)
    kept_swap.start()
    xs[:, :, :, 2 * W :] = jnp.zeros((2, 3, 3, WIDE // 2 - 2 * W, 2, 128), bf16)

    def row_valid(j6):
        return jnp.where(6 * m + j6 < H - pad_in[0], 1.0, 0.0).astype(f32)

    def field(v, t):
        return jnp.concatenate([xs.at[v, t, l].reshape(WIDE, 128)[...] for l in range(3)], axis=1)

    def send_chunk(phase, a):
        def one(i, carry):
            peer = lax.rem(m + i, CHIPS)
            pltpu.make_async_remote_copy(
                src_ref=send.at[phase, a, peer],
                dst_ref=got.at[phase, a, m],
                send_sem=ssem.at[phase, a],
                recv_sem=rsem.at[phase, a],
                device_id=(dp, 2 * peer + core),
                device_id_type=MESH,
            ).start()
            return carry

        lax.fori_loop(1, CHIPS, one, 0)

    def wait_chunk(phase, a, sem):
        whole = got.at[phase, a, pl.ds(0, 15)]
        pltpu.make_async_copy(whole, whole, sem.at[phase, a]).wait()

    def to_spectrum(v):
        line = lax.broadcasted_iota(jnp.int32, (256, HC), 0)
        second = lax.rem(line // 8, 2) == 1

        def one(a, carry):
            for t in range(3):
                result = dot(fts[v, a], field(v, t))
                result = result * jnp.where(second, row_valid(2 * t + 1), row_valid(2 * t))
                send[v, a, :, 16 * t : 16 * t + 16, :] = result.astype(bf16).reshape(16, 16, HC)
            send_chunk(v, a)
            got[v, a, m] = send[v, a, m]
            return carry

        lax.fori_loop(0, 3, one, 0)

    for v in range(2):
        for j in range(3):
            here, there = row_slots(v, 3 * core + j), row_slots(v, 3 * other + j)
            pltpu.make_async_copy(here, here, xown.at[v, j]).wait()
            pltpu.make_async_copy(there, there, xin_recv.at[v, j]).wait()
        tables[v].wait()
        to_spectrum(v)

    gacc[...] = jnp.zeros_like(gacc)
    bacc[...] = jnp.zeros_like(bacc)
    for copy in [kept_own, kept_swap] + tables[2:]:
        copy.wait()
    lane = lax.broadcasted_iota(jnp.int32, (BS, HC), 1)
    line = lax.broadcasted_iota(jnp.int32, (BS, HC), 0)
    for mat in range(2):
        for n in range(4):
            select = jnp.where(lane == line + BS * n, 1.0, 0.0).astype(bf16)
            real = dot(wraw[mat, 0, 4 * core + n], select)
            imag = dot(wraw[mat, 1, 4 * core + n], select)
            up, down = BS * n, HC + BS * n
            wd[mat, up : up + BS, :HC] = real.astype(bf16)
            wd[mat, up : up + BS, HC:] = imag.astype(bf16)
            wd[mat, down : down + BS, :HC] = (-imag).astype(bf16)
            wd[mat, down : down + BS, HC:] = real.astype(bf16)

    lane = lax.broadcasted_iota(jnp.int32, (NB, HC), 1)
    block = lax.broadcasted_iota(jnp.int32, (NB, HC), 0) - 4 * core
    spread = (lane >= BS * block) & (lane < BS * block + BS)
    for slot in range(6):
        bits = kraw[slot].astype(f32).astype(bf16)
        wide = lax.dot_general(
            bits,
            jnp.where(spread, 1.0, 0.0).astype(bf16),
            (((0,), (0,)), ((), ())),
            preferred_element_type=f32,
        )
        real_mode = jnp.where(6 * m + slot < W // 2 + 1, 1.0, 0.0).astype(f32)
        keeps[slot] = (wide * real_mode).astype(bf16)
    lane = lax.broadcasted_iota(jnp.int32, (BS, HC), 1)
    tiled = sum(jnp.where(lane == line + BS * n, 1.0, 0.0).astype(f32) for n in range(4))
    for mat, ref in enumerate((b_one, b_two)):
        for p in range(2):
            copies = jnp.dot(
                ref[p], tiled, precision=lax.Precision.HIGHEST, preferred_element_type=f32
            )
            brow[mat, p] = jnp.where(spread, copies, 0.0).sum(0, keepdims=True)

    def spectral(phase, a, half):
        held = got[phase, a].reshape(768, HC)
        return dot(lfs[half * HC : half * HC + HC, :], held)

    def unspectral(phase, a):
        for t in range(2):
            result = dot(lis[t * HC : t * HC + HC, :], fil[...]).astype(bf16)
            send[phase, a, 8 * t : 8 * t + 8] = result.reshape(8, 48, HC)
        got[phase, a, m] = send[phase, a, m]

    def product(left, mat):
        for n in range(3):
            tmp[:, 256 * n : 256 * n + 256] = dot(left, wd[mat, :, 256 * n : 256 * n + 256])

    def product_turned(left, mat):
        for n in range(3):
            tmp[:, 256 * n : 256 * n + 256] = lax.dot_general(
                left,
                wd[mat, 256 * n : 256 * n + 256, :],
                (((1,), (1,)), ((), ())),
                preferred_element_type=f32,
            )

    def rows_of(step):
        return pl.ds(pl.multiple_of(step * 32, 32), 32)

    def kept_rows(a, step):
        kk = lax.rem(step // 3, 2)
        q = pl.multiple_of(lax.rem(step, 3) * 32, 32)
        return keeps[2 * a + kk, pl.ds(q, 32), :].astype(f32)

    def forward(a, carry):
        wait_chunk(0, a, rsem)
        for p in range(2):
            spec[a, :, p * HC : p * HC + HC] = spectral(0, a, p).astype(bf16)
        product(spec[a], 0)

        def gelu_rows(step, carry):
            rows = rows_of(step)
            for p in range(2):
                part = slice(p * HC, p * HC + HC)
                value, tilt = gelu_both(tmp[rows, part] + brow[0, p])
                hid[a, rows, part] = value.astype(bf16)
                slope[a, rows, part] = tilt
            return carry

        lax.fori_loop(0, 12, gelu_rows, 0)
        product(hid[a], 1)

        def shrink_rows(step, carry):
            rows = rows_of(step)
            kept = kept_rows(a, step)
            for p in range(2):
                part = slice(p * HC, p * HC + HC)
                value = tmp[rows, part] + brow[1, p]
                tangent = jnp.tanh(value * (1.0 / shrink))
                filtered = (value - shrink * tangent) * kept
                fil[pl.ds(pl.multiple_of(p * HC + step * 32, 32), 32), :] = filtered.astype(bf16)
                kt[a, rows, part] = kept * (tangent * tangent)
            return carry

        lax.fori_loop(0, 12, shrink_rows, 0)
        unspectral(2, a)
        return carry

    lax.fori_loop(0, 3, forward, 0)
    send_chunk(2, 0)

    def add_grad(mat, left, right):
        for n in range(3):
            part = slice(256 * n, 256 * n + 256)
            gacc[mat, :, part] += lax.dot_general(
                left, right[:, part], (((0,), (0,)), ((), ())), preferred_element_type=f32
            )

    def backward(a, carry):
        wait_chunk(1, a, rsem)
        for p in range(2):
            tmp[:, p * HC : p * HC + HC] = spectral(1, a, p)

        def scaled_rows(mat, scale):
            def one(step, carry):
                rows = rows_of(step)
                for p in range(2):
                    part = slice(p * HC, p * HC + HC)
                    value = (tmp[rows, part] * scale[a, rows, part]).astype(bf16)
                    dtwo[rows, part] = value
                    bacc[mat, :, part] += value.astype(f32).reshape(4, 8, HC).sum(0)
                return carry

            lax.fori_loop(0, 12, one, 0)

        scaled_rows(1, kt)
        add_grad(1, hid[a], dtwo[...])
        product_turned(dtwo[...], 1)
        scaled_rows(0, slope)
        add_grad(0, spec[a], dtwo[...])
        product_turned(dtwo[...], 0)
        for p in range(2):
            fil[p * HC : p * HC + HC, :] = tmp[:, p * HC : p * HC + HC].astype(bf16)
        unspectral(3, a)
        return carry

    lax.fori_loop(0, 3, backward, 0)

    gp[:, :, 104:, :] = jnp.zeros((4, 4, 24, 128), f32)
    for mat in range(2):
        for n in range(4):
            start = BS * n // 128 * 128
            shift = BS * n - start
            window = 256 if shift + BS > 128 else 128
            up = slice(BS * n, BS * n + BS)
            down = slice(HC + BS * n, HC + BS * n + BS)
            left = slice(start, start + window)
            right = slice(HC + start, HC + start + window)

            def align(value):
                if shift:
                    value = pltpu.roll(value, window - shift, 1)
                return value[:, :128]

            gp[n, 2 * mat, :BS, :] = align(gacc[mat, up, left] + gacc[mat, down, right])
            gp[n, 2 * mat + 1, :BS, :] = align(gacc[mat, up, right] - gacc[mat, down, left])
            gp[n, 2 * mat, BS:104, :] = align(bacc[mat, :, left])
            gp[n, 2 * mat + 1, BS:104, :] = align(bacc[mat, :, right])

    def gather(count, source, target, device, at):
        def one(i, carry):
            pltpu.make_async_remote_copy(
                src_ref=source(i),
                dst_ref=target,
                send_sem=gsend.at[at],
                recv_sem=grecv.at[at],
                device_id=device(i),
                device_id_type=MESH,
            ).start()
            return carry

        lax.fori_loop(1, count + 1, one, 0)

    def settle(part, at):
        pltpu.make_async_copy(part, part, grecv.at[at]).wait()

    def depth_of(i):
        return lax.rem(depth + i, 8)

    def depth_device(i):
        at = depth_of(i)
        return (4 * (at // 4) + x, 2 * (y * 4 + lax.rem(at, 4)) + core)

    def depth_rows(i):
        return pl.ds(pl.multiple_of(16 * i, 16), 16)

    gather(
        15,
        lambda i: gp.at[lax.rem(y + i // 4, 4), lax.rem(x + lax.rem(i, 4), 4)],
        gr.at[4 * y + x],
        plane_device,
        0,
    )
    send_chunk(2, 1)
    gr[4 * y + x] = gp[y, x]
    settle(gr.at[pl.ds(0, 15)], 0)
    total = gr[0]
    for i in range(1, 16):
        total = total + gr[i]
    s_two[...] = total
    gather(7, lambda i: s_two.at[depth_rows(depth_of(i))], gz.at[depth], depth_device, 1)
    send_chunk(2, 2)
    gz[depth] = s_two[depth_rows(depth), :]
    settle(gz.at[pl.ds(0, 7)], 1)
    total = gz[0]
    for i in range(1, 8):
        total = total + gz[i]
    s_three[...] = total * (1.0 / (IMAGES * H))
    gather(7, lambda i: s_three, fin.at[depth], depth_device, 2)
    send_chunk(3, 0)
    fin[depth] = s_three[...]
    settle(fin.at[pl.ds(0, 7)], 2)
    fy[y, x] = fin[...].reshape(128, 128)
    gather(15, lambda i: fy.at[y, x], fy.at[y, x], plane_device, 3)
    send_chunk(3, 1)
    settle(gr.at[pl.ds(0, 15)], 3)
    gather(1, lambda i: fy, fc, lambda i: buddy, 4)
    send_chunk(3, 2)

    def leave(v):
        ref = (out_x, out_c)[v]

        def add(t, a):
            piece = got[2 + v, a, :, pl.ds(pl.multiple_of(16 * t, 16), 16), :]
            piece = piece.reshape(256, HC)
            for n in range(4):
                rows = slice(n * 192, n * 192 + 192)
                facc[t, rows, :] += dot(tts[1 - v, a, rows, :], piece)

        def begin(t, carry):
            for l in range(3):
                part = xs.at[v, t, l].reshape(WIDE, 128)[...]
                facc[t, :, 128 * l : 128 * l + 128] = part.astype(f32)
            return carry

        lax.fori_loop(0, 3, begin, 0)
        for a in range(2):
            wait_chunk(2 + v, a, rsem)

            def one(t, carry):
                add(t, a)
                return carry

            lax.fori_loop(0, 3, one, 0)
        wait_chunk(2 + v, 2, rsem)

        def away(j6):
            j = j6 - 3 * other
            for l in range(3):
                pltpu.make_async_remote_copy(
                    src_ref=row_slot(v, j6, l),
                    dst_ref=ref.at[j, :, :, tile(core, l)],
                    send_sem=osend.at[v, j],
                    recv_sem=orecv.at[v, j],
                    device_id=buddy,
                    device_id_type=MESH,
                ).start()

        def stay(j6):
            j = j6 - 3 * core
            for l in range(3):
                pltpu.make_async_copy(
                    row_slot(v, j6, l), ref.at[j, :, :, tile(core, l)], oloc.at[v, j]
                ).start()

        for step in range(3):
            t = step * core + (2 - step) * other
            add(t, 2)
            for jj in range(2):
                rows = slice(jj * 2 * W, jj * 2 * W + 2 * W)
                scale = row_valid(2 * t + jj)
                for l in range(3):
                    part = facc[t, rows, 128 * l : 128 * l + 128] * scale
                    xs.at[v, t, l].reshape(WIDE, 128)[rows, :] = part.astype(bf16)
            if step == 0:
                away(2 * t)
                away(2 * t + 1)
            elif step == 1:
                away(2 * t + other)
                stay(2 * t + core)
            else:
                stay(2 * t)
                stay(2 * t + 1)

    def left(v):
        ref = (out_x, out_c)[v]
        for j in range(3):
            gone, arrived = ref.at[j, :, :, mine], ref.at[j, :, :, theirs]
            pltpu.make_async_copy(gone, gone, oloc.at[v, j]).wait()
            pltpu.make_async_copy(arrived, arrived, orecv.at[v, j]).wait()
            pltpu.make_async_copy(gone, gone, osend.at[v, j]).wait()

    mine = pl.ds(pl.multiple_of(core * HC, 128), HC)
    theirs = pl.ds(pl.multiple_of(other * HC, 128), HC)
    leave(0)

    settle(fc, 4)
    for half, held in ((core, fy), (other, fc)):

        def one(n, carry):
            for mat, (weight, bias) in enumerate(((gw_one, gb_one), (gw_two, gb_two))):
                for p in range(2):
                    weight[p, 4 * half + n] = held[n, 2 * mat + p, :BS, :BS]
                    bias[p, 4 * half + n] = held[n, 2 * mat + p, BS:104, :BS].sum(0, keepdims=True)
            return carry

        lax.fori_loop(0, 4, one, 0)

    leave(1)

    def sent(i, carry):
        wait_chunk(i // 3, lax.rem(i, 3), ssem)
        return carry

    lax.fori_loop(0, 12, sent, 0)
    for v in range(2):
        for j in range(3):
            there = row_slots(v, 3 * core + j)
            pltpu.make_async_copy(there, there, xin_send.at[v, j]).wait()
    for at, part in (
        (0, gr.at[pl.ds(0, 15)]),
        (1, gz.at[pl.ds(0, 7)]),
        (2, fin.at[pl.ds(0, 7)]),
        (3, gr.at[pl.ds(0, 15)]),
        (4, fc),
    ):
        pltpu.make_async_copy(part, part, gsend.at[at]).wait()
    left(0)
    left(1)


def mix(x_wide, c_wide, kept, pad_rows, w_one, w_two, b_one, b_two):
    forward_lon, inverse_lon = longitude_parts()
    ahead = np.stack([to_spectrum_table(forward_lon), to_spectrum_table(inverse_lon)])
    lf, li = lat_tables()
    as_bf16 = lambda table: jnp.asarray(table.astype(jnp.bfloat16))
    tables = (as_bf16(ahead), as_bf16(ahead.transpose(0, 1, 3, 2)), as_bf16(lf), as_bf16(li))
    anywhere = pl.BlockSpec(memory_space=pl.ANY)
    vmem = pl.BlockSpec(memory_space=pltpu.VMEM)
    dma = pltpu.SemaphoreType.DMA
    return pl.pallas_call(
        kernel,
        out_shape=(
            jax.ShapeDtypeStruct(x_wide.shape, bf16),
            jax.ShapeDtypeStruct(c_wide.shape, bf16),
            jax.ShapeDtypeStruct((2, NB, BS, BS), f32),
            jax.ShapeDtypeStruct((2, NB, 1, BS), f32),
            jax.ShapeDtypeStruct((2, NB, BS, BS), f32),
            jax.ShapeDtypeStruct((2, NB, 1, BS), f32),
        ),
        in_specs=[anywhere] * 3
        + [pl.BlockSpec(memory_space=pltpu.SMEM)]
        + [anywhere] * 2
        + [vmem] * 2
        + [anywhere] * 4,
        out_specs=(anywhere, anywhere, vmem, vmem, vmem, vmem),
        scratch_shapes=[
            pltpu.VMEM((2, 3, 3, WIDE // 2, 2, 128), bf16),
            pltpu.VMEM((2, 3, 256, WIDE), bf16),
            pltpu.VMEM((2, 3, WIDE, 256), bf16),
            pltpu.VMEM((768, 768), bf16),
            pltpu.VMEM((768, 768), bf16),
            pltpu.VMEM((2, 2, NB, BS, BS), bf16),
            pltpu.VMEM((2, 768, 768), bf16),
            pltpu.VMEM((6, NB, H), jnp.int32),
            pltpu.VMEM((6, H, HC), bf16),
            pltpu.VMEM((2, 2, 1, HC), f32),
            pltpu.VMEM((4, 3, CHIPS, 48, HC), bf16),
            pltpu.VMEM((4, 3, CHIPS, 48, HC), bf16),
            pltpu.VMEM((3, WIDE, HC), f32),
            pltpu.VMEM((3, HC, 768), bf16),
            pltpu.VMEM((3, HC, 768), bf16),
            pltpu.VMEM((3, HC, 768), f32),
            pltpu.VMEM((3, HC, 768), f32),
            pltpu.VMEM((HC, 768), f32),
            pltpu.VMEM((768, HC), bf16),
            pltpu.VMEM((HC, 768), bf16),
            pltpu.VMEM((2, 768, 768), f32),
            pltpu.VMEM((2, 8, 768), f32),
            pltpu.VMEM((4, 4, 128, 128), f32),
            pltpu.VMEM((16, 128, 128), f32),
            pltpu.VMEM((128, 128), f32),
            pltpu.VMEM((8, 16, 128), f32),
            pltpu.VMEM((16, 128), f32),
            pltpu.VMEM((8, 16, 128), f32),
            pltpu.VMEM((4, 4, 128, 128), f32),
            pltpu.VMEM((4, 4, 128, 128), f32),
            dma((8,)),
            dma((2, 3)),
            dma((3, 3)),
            dma((3, 3)),
            dma((4, 3)),
            dma((4, 3)),
            dma((2, 3)),
            dma((2, 3)),
            dma((2, 3)),
            dma((5,)),
            dma((5,)),
        ],
        compiler_params=pltpu.CompilerParams(
            collective_id=0, has_side_effects=True, vmem_limit_bytes=61 * 2**20
        ),
    )(x_wide, c_wide, kept, pad_rows, w_one, w_two, b_one, b_two, *tables)


def on_device(inputs, cotangent, kept_modes, pad_rows, weight_one, bias_one, weight_two, bias_two):
    wide = lambda array: jnp.transpose(array, (1, 2, 0, 3))
    out_x, out_c, gw_one, gb_one, gw_two, gb_two = mix(
        wide(inputs),
        wide(cotangent),
        jnp.transpose(kept_modes, (2, 0, 1)),
        pad_rows,
        weight_one,
        weight_two,
        bias_one,
        bias_two,
    )
    narrow = lambda array: jnp.transpose(array, (2, 0, 1, 3))
    return narrow(out_x), narrow(out_c), gw_one, gb_one[:, :, 0], gw_two, gb_two[:, :, 0]


def solution(mesh):
    placed = (
        P("dp", "space", None, None),
        P("dp", "space", None, None),
        P(None, None, "space"),
        P(),
        P(),
        P(),
        P(),
        P(),
    )
    return jax.shard_map(
        on_device,
        mesh=mesh,
        in_specs=placed,
        out_specs=(P("dp", "space", None, None), P("dp", "space", None, None), P(), P(), P(), P()),
        check_vma=False,
    )
```

time: 207 us -> 195 us (0.942)
  local copies, waits for them, and re-layouts: 14.5 us -> 8.49 us
  other arithmetic: 4.96 us -> 0 us
    mul x2 -> x0, other arithmetic: 4.17 us -> none  [the longest x1 2.26 us: on_device(): out_c[:, :, :W] * valid]
    pad x2 -> x0, local copies, waits for them, and re-layouts: 2.67 us -> none  [the longest x1 1.35 us: on_device(): x_pad = jnp.pad(inputs * valid, margin)]
where the time goes in v2:
time: 195 us
  Pallas kernels  185 us (95%)
  local copies, waits for them, and re-layouts  8.49 us (4%)
    pallas_call x1, Pallas kernels, mix(): pl.pallas_call(kernel, out_shape=(jax.ShapeDtypeStruct(x_wide.shape, bf16...  185 us
    unnamed x16, local copies, waits for them, and re-layouts  8.49 us

profile of v2, /device:TPU:1, one launch (start us, length us, event | category | flops | bytes accessed | tf_op | source)
XLA Modules:
  0.0 195.0 jit_solution(15542713318532012797)
XLA Ops:
  1.3 185.2 %shard_map.163 = (bf16[3,180,2,768]{3,2,1,0:T(2,128)(2,1)}, bf16[3,180,2,768]{3,2,1,0:T(2,128)(2,1)}, f32[2,8,96,96]{3,2,1,0:T(8,128)}, f32[2,8,1,96]{3,2,1,0:T(...) custom-call(bf16[3,180,2,768]{3,2,1,0:T(2,128)(2,1)} %bitcast.9, bf16[3,180,2,768]{3,2,1,0:T(2,128)(2,1)} %bitcast.10, ...), custom_call_target="tpu_custom_call" | custom-call | tf_op jit(solution)/shard_map/pallas_call | solution.py:587
  186.5 0.0 copy-start
  186.5 3.9 %copy.25 = bf16[2,3,180,768]{3,0,2,1:T(2,128)(2,1)} copy(bf16[2,3,180,768]{3,0,2,1:T(2,128)(2,1)} %bitcast.8) | data formatting | bytes 3317760
  190.3 0.0 copy-done
  190.3 0.0 copy-start.2
  190.3 0.0 copy-start.4
  190.3 0.0 copy-start.1
  190.4 1.2 copy.26
  191.5 0.5 copy-done.2
  192.0 0.0 copy-start.3
  192.0 0.9 copy.27
  192.9 0.0 copy-done.4
  192.9 0.6 copy.28
  193.5 0.0 copy-done.1
  193.5 0.9 copy.29
  194.4 0.0 copy-done.3
  194.4 0.6 copy.30
Async XLA Ops:
  186.5 3.9 %copy-start = (bf16[3,180,2,768]{3,2,1,0:T(2,128)(2,1)S(1)}, bf16[3,180,2,768]{3,2,1,0:T(2,128)(2,1)}, u32[]{:S(2)}) copy-start(bf16[3,180,2,768]{3,2,1,0:T(2,128)(2,1)} %get-tuple-element.13) | copy-start | bytes 4976644
  190.3 1.7 copy-start.2
  190.3 2.5 %copy-start.4 = (f32[2,8,1,96]{3,2,1,0:T(1,128)S(1)}, f32[2,8,1,96]{3,2,1,0:T(1,128)}, u32[]{:S(2)}) copy-start(f32[2,8,1,96]{3,2,1,0:T(1,128)} %get-tuple-element.15) | copy-start | bytes 18436
  190.3 3.1 %copy-start.1 = (f32[2,8,96,96]{3,2,1,0:T(8,128)S(1)}, f32[2,8,96,96]{3,2,1,0:T(8,128)}, u32[]{:S(2)}) copy-start(f32[2,8,96,96]{3,2,1,0:T(8,128)} %get-tuple-element.28) | copy-start | bytes 1769476
  192.0 2.4 %copy-start.3 = (f32[2,8,1,96]{3,2,1,0:T(1,128)S(1)}, f32[2,8,1,96]{3,2,1,0:T(1,128)}, u32[]{:S(2)}) copy-start(f32[2,8,1,96]{3,2,1,0:T(1,128)} %get-tuple-element.17) | copy-start | bytes 18436

commit v3 on v2

--- a/solution.py
+++ b/solution.py
@@ -88,11 +88,11 @@
 
 def kernel(
     x_in, c_in, kept_in, pad_in, w_one, w_two, b_one, b_two, ft_in, tt_in, lf_in, li_in,
-    out_x, out_c, gw_one, gb_one, gw_two, gb_two,
+    out_x, out_c, out_g,
     xs, fts, tts, lfs, lis, wraw, wd, kraw, keeps, brow,
     send, got, facc, spec, hid, slope, kt, tmp, fil, dtwo, gacc, bacc,
-    gp, gr, s_two, gz, s_three, fin, fy, fc,
-    load_sem, xown, xin_send, xin_recv, ssem, rsem, oloc, osend, orecv, gsend, grecv,
+    gp, gr, s_two, gz, s_three, fin, fy,
+    load_sem, xown, xin_send, xin_recv, ssem, rsem, oloc, osend, orecv, gsend, grecv, gloc,
 ):
     me = lax.axis_index("space")
     dp = lax.axis_index("dp")
@@ -196,7 +196,7 @@
     def field(v, t):
         return jnp.concatenate([xs.at[v, t, l].reshape(WIDE, 128)[...] for l in range(3)], axis=1)
 
-    def send_chunk(phase, a):
+    def send_chunk(phase, a, first=1, last=CHIPS, beside=None):
         def one(i, carry):
             peer = lax.rem(m + i, CHIPS)
             pltpu.make_async_remote_copy(
@@ -207,9 +207,11 @@
                 device_id=(dp, 2 * peer + core),
                 device_id_type=MESH,
             ).start()
+            if beside is not None:
+                beside(i)
             return carry
 
-        lax.fori_loop(1, CHIPS, one, 0)
+        lax.fori_loop(first, last, one, 0)
 
     def wait_chunk(phase, a, sem):
         whole = got.at[phase, a, pl.ds(0, 15)]
@@ -344,6 +346,7 @@
 
     lax.fori_loop(0, 3, forward, 0)
     send_chunk(2, 0)
+    send_chunk(2, 1, 1, 8)
 
     def add_grad(mat, left, right):
         for n in range(3):
@@ -382,7 +385,7 @@
 
     lax.fori_loop(0, 3, backward, 0)
 
-    gp[:, :, 104:, :] = jnp.zeros((4, 4, 24, 128), f32)
+    first_row = lax.broadcasted_iota(jnp.int32, (128 - BS, 128), 0) == 0
     for mat in range(2):
         for n in range(4):
             start = BS * n // 128 * 128
@@ -398,24 +401,28 @@
                     value = pltpu.roll(value, window - shift, 1)
                 return value[:, :128]
 
-            gp[n, 2 * mat, :BS, :] = align(gacc[mat, up, left] + gacc[mat, down, right])
-            gp[n, 2 * mat + 1, :BS, :] = align(gacc[mat, up, right] - gacc[mat, down, left])
-            gp[n, 2 * mat, BS:104, :] = align(bacc[mat, :, left])
-            gp[n, 2 * mat + 1, BS:104, :] = align(bacc[mat, :, right])
-
-    def gather(count, source, target, device, at):
+            gp[n, 2 * mat, :BS, :] = align(gacc[mat, up, left] + gacc[mat, down, right]).astype(bf16)
+            gp[n, 2 * mat + 1, :BS, :] = align(gacc[mat, up, right] - gacc[mat, down, left]).astype(bf16)
+            for p, part in enumerate((left, right)):
+                summed = align(bacc[mat, :, part]).sum(0, keepdims=True)
+                gp[n, 2 * mat + p, BS:, :] = jnp.where(first_row, summed, 0.0).astype(bf16)
+
+    def message(i, source, target, device, at):
+        pltpu.make_async_remote_copy(
+            src_ref=source,
+            dst_ref=target,
+            send_sem=gsend.at[at],
+            recv_sem=grecv.at[at],
+            device_id=device,
+            device_id_type=MESH,
+        ).start()
+
+    def to_depths(source, target, at):
         def one(i, carry):
-            pltpu.make_async_remote_copy(
-                src_ref=source(i),
-                dst_ref=target,
-                send_sem=gsend.at[at],
-                recv_sem=grecv.at[at],
-                device_id=device(i),
-                device_id_type=MESH,
-            ).start()
+            message(i, source(i), target, depth_device(i), at)
             return carry
 
-        lax.fori_loop(1, count + 1, one, 0)
+        lax.fori_loop(1, 8, one, 0)
 
     def settle(part, at):
         pltpu.make_async_copy(part, part, grecv.at[at]).wait()
@@ -430,38 +437,36 @@
     def depth_rows(i):
         return pl.ds(pl.multiple_of(16 * i, 16), 16)
 
-    gather(
-        15,
-        lambda i: gp.at[lax.rem(y + i // 4, 4), lax.rem(x + lax.rem(i, 4), 4)],
-        gr.at[4 * y + x],
-        plane_device,
-        0,
-    )
-    send_chunk(2, 1)
+    def to_owner(i):
+        row, column = lax.rem(y + i // 4, 4), lax.rem(x + lax.rem(i, 4), 4)
+        message(i, gp.at[row, column], gr.at[4 * y + x], plane_device(i), 0)
+
+    def from_owner(i):
+        message(i, fy.at[y, x], fy.at[y, x], plane_device(i), 3)
+
+    lax.fori_loop(1, 8, lambda i, carry: (to_owner(i), carry)[1], 0)
+    send_chunk(2, 1, 8, CHIPS, to_owner)
+    send_chunk(2, 2)
     gr[4 * y + x] = gp[y, x]
     settle(gr.at[pl.ds(0, 15)], 0)
-    total = gr[0]
+    total = gr[0].astype(f32)
     for i in range(1, 16):
-        total = total + gr[i]
+        total = total + gr[i].astype(f32)
     s_two[...] = total
-    gather(7, lambda i: s_two.at[depth_rows(depth_of(i))], gz.at[depth], depth_device, 1)
-    send_chunk(2, 2)
+    to_depths(lambda i: s_two.at[depth_rows(depth_of(i))], gz.at[depth], 1)
+    send_chunk(3, 0)
     gz[depth] = s_two[depth_rows(depth), :]
     settle(gz.at[pl.ds(0, 7)], 1)
     total = gz[0]
     for i in range(1, 8):
         total = total + gz[i]
     s_three[...] = total * (1.0 / (IMAGES * H))
-    gather(7, lambda i: s_three, fin.at[depth], depth_device, 2)
-    send_chunk(3, 0)
+    to_depths(lambda i: s_three, fin.at[depth], 2)
+    send_chunk(3, 1)
     fin[depth] = s_three[...]
     settle(fin.at[pl.ds(0, 7)], 2)
-    fy[y, x] = fin[...].reshape(128, 128)
-    gather(15, lambda i: fy.at[y, x], fy.at[y, x], plane_device, 3)
-    send_chunk(3, 1)
-    settle(gr.at[pl.ds(0, 15)], 3)
-    gather(1, lambda i: fy, fc, lambda i: buddy, 4)
-    send_chunk(3, 2)
+    fy[y, x] = fin[...].reshape(128, 128).astype(bf16)
+    send_chunk(3, 2, 1, CHIPS, from_owner)
 
     def leave(v):
         ref = (out_x, out_c)[v]
@@ -540,17 +545,18 @@
     theirs = pl.ds(pl.multiple_of(other * HC, 128), HC)
     leave(0)
 
-    settle(fc, 4)
-    for half, held in ((core, fy), (other, fc)):
-
-        def one(n, carry):
-            for mat, (weight, bias) in enumerate(((gw_one, gb_one), (gw_two, gb_two))):
-                for p in range(2):
-                    weight[p, 4 * half + n] = held[n, 2 * mat + p, :BS, :BS]
-                    bias[p, 4 * half + n] = held[n, 2 * mat + p, BS:104, :BS].sum(0, keepdims=True)
-            return carry
-
-        lax.fori_loop(0, 4, one, 0)
+    settle(gr.at[pl.ds(0, 15)], 3)
+    fy_away = pltpu.make_async_remote_copy(
+        src_ref=fy,
+        dst_ref=out_g.at[core],
+        send_sem=gsend.at[4],
+        recv_sem=grecv.at[4],
+        device_id=buddy,
+        device_id_type=MESH,
+    )
+    fy_away.start()
+    fy_stays = pltpu.make_async_copy(fy, out_g.at[core], gloc)
+    fy_stays.start()
 
     leave(1)
 
@@ -568,11 +574,12 @@
         (1, gz.at[pl.ds(0, 7)]),
         (2, fin.at[pl.ds(0, 7)]),
         (3, gr.at[pl.ds(0, 15)]),
-        (4, fc),
     ):
         pltpu.make_async_copy(part, part, gsend.at[at]).wait()
     left(0)
     left(1)
+    fy_away.wait()
+    fy_stays.wait()
 
 
 def mix(x_wide, c_wide, kept, pad_rows, w_one, w_two, b_one, b_two):
@@ -589,17 +596,14 @@
         out_shape=(
             jax.ShapeDtypeStruct(x_wide.shape, bf16),
             jax.ShapeDtypeStruct(c_wide.shape, bf16),
-            jax.ShapeDtypeStruct((2, NB, BS, BS), f32),
-            jax.ShapeDtypeStruct((2, NB, 1, BS), f32),
-            jax.ShapeDtypeStruct((2, NB, BS, BS), f32),
-            jax.ShapeDtypeStruct((2, NB, 1, BS), f32),
+            jax.ShapeDtypeStruct((2, 4, 4, 128, 128), bf16),
         ),
         in_specs=[anywhere] * 3
         + [pl.BlockSpec(memory_space=pltpu.SMEM)]
         + [anywhere] * 2
         + [vmem] * 2
         + [anywhere] * 4,
-        out_specs=(anywhere, anywhere, vmem, vmem, vmem, vmem),
+        out_specs=(anywhere, anywhere, anywhere),
         scratch_shapes=[
             pltpu.VMEM((2, 3, 3, WIDE // 2, 2, 128), bf16),
             pltpu.VMEM((2, 3, 256, WIDE), bf16),
@@ -623,14 +627,13 @@
             pltpu.VMEM((HC, 768), bf16),
             pltpu.VMEM((2, 768, 768), f32),
             pltpu.VMEM((2, 8, 768), f32),
-            pltpu.VMEM((4, 4, 128, 128), f32),
-            pltpu.VMEM((16, 128, 128), f32),
+            pltpu.VMEM((4, 4, 128, 128), bf16),
+            pltpu.VMEM((16, 128, 128), bf16),
             pltpu.VMEM((128, 128), f32),
             pltpu.VMEM((8, 16, 128), f32),
             pltpu.VMEM((16, 128), f32),
             pltpu.VMEM((8, 16, 128), f32),
-            pltpu.VMEM((4, 4, 128, 128), f32),
-            pltpu.VMEM((4, 4, 128, 128), f32),
+            pltpu.VMEM((4, 4, 128, 128), bf16),
             dma((8,)),
             dma((2, 3)),
             dma((3, 3)),
@@ -642,6 +645,7 @@
             dma((2, 3)),
             dma((5,)),
             dma((5,)),
+            dma,
         ],
         compiler_params=pltpu.CompilerParams(
             collective_id=0, has_side_effects=True, vmem_limit_bytes=61 * 2**20
@@ -649,20 +653,80 @@
     )(x_wide, c_wide, kept, pad_rows, w_one, w_two, b_one, b_two, *tables)
 
 
+def finish(
+    x_ref, c_ref, g_ref, out_x, out_c, gw_one, gb_one, gw_two, gb_two,
+    held, parts, weights, biases, in_sem, out_sem, g_sem,
+):
+    loads, stores = [], []
+    for v, (source, target) in enumerate(((x_ref, out_x), (c_ref, out_c))):
+        for j in range(3):
+            loads.append(pltpu.make_async_copy(source.at[j], held.at[v, j], in_sem.at[v, j]))
+            stores.append(pltpu.make_async_copy(held.at[v, j], target.at[j], out_sem.at[v, j]))
+    load_parts = pltpu.make_async_copy(g_ref, parts, g_sem.at[0])
+    load_parts.start()
+    for copy in loads:
+        copy.start()
+    load_parts.wait()
+    for mat, (weight, bias) in enumerate(((gw_one, gb_one), (gw_two, gb_two))):
+        for p in range(2):
+            for n in range(NB):
+                block = parts[n // 4, n % 4, 2 * mat + p].astype(f32)
+                weights[mat, p, n] = block[:BS, :BS]
+                biases[mat, p, n : n + 1, :] = block[BS : BS + 1, :BS]
+        stores.append(pltpu.make_async_copy(weights.at[mat], weight, g_sem.at[1 + mat]))
+        stores[-1].start()
+        stores.append(pltpu.make_async_copy(biases.at[mat], bias, g_sem.at[3 + mat]))
+        stores[-1].start()
+    for load, store in zip(loads, stores):
+        load.wait()
+        store.start()
+    for store in stores:
+        store.wait()
+
+
+def settle_outputs(out_x, out_c, out_g):
+    anywhere = pl.BlockSpec(memory_space=pl.ANY)
+    return pl.pallas_call(
+        finish,
+        out_shape=(
+            jax.ShapeDtypeStruct(out_x.shape, bf16),
+            jax.ShapeDtypeStruct(out_c.shape, bf16),
+            jax.ShapeDtypeStruct((2, NB, BS, BS), f32),
+            jax.ShapeDtypeStruct((2, NB, BS), f32),
+            jax.ShapeDtypeStruct((2, NB, BS, BS), f32),
+            jax.ShapeDtypeStruct((2, NB, BS), f32),
+        ),
+        in_specs=[anywhere] * 3,
+        out_specs=(anywhere,) * 6,
+        scratch_shapes=[
+            pltpu.VMEM((2,) + out_x.shape, bf16),
+            pltpu.VMEM(out_g.shape, bf16),
+            pltpu.VMEM((2, 2, NB, BS, BS), f32),
+            pltpu.VMEM((2, 2, NB, BS), f32),
+            pltpu.SemaphoreType.DMA((2, 3)),
+            pltpu.SemaphoreType.DMA((2, 3)),
+            pltpu.SemaphoreType.DMA((5,)),
+        ],
+        compiler_params=pltpu.CompilerParams(vmem_limit_bytes=60 * 2**20),
+    )(out_x, out_c, out_g)
+
+
 def on_device(inputs, cotangent, kept_modes, pad_rows, weight_one, bias_one, weight_two, bias_two):
     wide = lambda array: jnp.transpose(array, (1, 2, 0, 3))
-    out_x, out_c, gw_one, gb_one, gw_two, gb_two = mix(
-        wide(inputs),
-        wide(cotangent),
-        jnp.transpose(kept_modes, (2, 0, 1)),
-        pad_rows,
-        weight_one,
-        weight_two,
-        bias_one,
-        bias_two,
+    out_x, out_c, gw_one, gb_one, gw_two, gb_two = settle_outputs(
+        *mix(
+            wide(inputs),
+            wide(cotangent),
+            jnp.transpose(kept_modes, (2, 0, 1)),
+            pad_rows,
+            weight_one,
+            weight_two,
+            bias_one,
+            bias_two,
+        )
     )
     narrow = lambda array: jnp.transpose(array, (2, 0, 1, 3))
-    return narrow(out_x), narrow(out_c), gw_one, gb_one[:, :, 0], gw_two, gb_two[:, :, 0]
+    return narrow(out_x), narrow(out_c), gw_one, gb_one, gw_two, gb_two
 
 
 def solution(mesh):

time: 195 us -> 181 us (0.928)
  local copies, waits for them, and re-layouts: 8.49 us -> 0 us
  Pallas kernels: 185 us -> 178 us
    pallas_call x1, Pallas kernels: 185 us -> 174 us  [mix(): pl.pallas_call(kernel, out_shape=(jax.ShapeDtypeStruct(x_wide.shape, bf16...]
    unnamed x16 -> x0, local copies, waits for them, and re-layouts: 8.49 us -> none
    pallas_call x0 -> x1, Pallas kernels: none -> 4.51 us  [settle_outputs(): pl.pallas_call(finish, out_shape=(jax.ShapeDtypeStruct(out_x.shape, bf16)...]
where the time goes in v3:
time: 181 us; the launch traced here: 180 us
  Pallas kernels  178 us (98%)
    pallas_call x1, Pallas kernels, mix(): pl.pallas_call(kernel, out_shape=(jax.ShapeDtypeStruct(x_wide.shape, bf16...  174 us
    pallas_call x1, Pallas kernels, settle_outputs(): pl.pallas_call(finish, out_shape=(jax.ShapeDtypeStruct(out_x.shape, bf16)...  4.51 us

profile of v3, /device:TPU:1, one launch (start us, length us, event | category | flops | bytes accessed | tf_op | source)
XLA Modules:
  0.0 179.9 jit_solution(9395527299617139269)
XLA Ops:
  1.3 173.9 %shard_map.163 = (bf16[3,180,2,768]{3,2,1,0:T(2,128)(2,1)}, bf16[3,180,2,768]{3,2,1,0:T(2,128)(2,1)}, bf16[2,4,4,128,128]{4,3,2,1,0:T(8,128)(2,1)}) custom-call(bf16[3,180,2,768]{3,2,1,0:T(2,128)(2,1)} %bitcast.5, bf16[3,180,2,768]{3,2,1,0:T(2,128)(2,1)} %bitcast.6, s32[3,8,96]{2,1,0:T(8,128)} %bitcast.7, s32[1]{0:T(128)S(6)} %copy.18.pad_in, ...), custom_call_target="tpu_custom_call" | custom-call | tf_op jit(solution)/shard_map/pallas_call | solution.py:594
  175.2 4.5 %shard_map.164 = (bf16[3,180,2,768]{3,2,1,0:T(2,128)(2,1)}, bf16[3,180,2,768]{3,2,1,0:T(2,128)(2,1)}, f32[2,8,96,96]{3,2,1,0:T(8,128)}, f32[2,8,96]{2,1,0:T(8,12...) custom-call(bf16[3,180,2,768]{3,2,1,0:T(2,128)(2,1)} %get-tuple-element.15.x_ref, ...), custom_call_target="tpu_custom_call" | custom-call | tf_op jit(solution)/shard_map/pallas_call | solution.py:689

commit v4 on v3

--- a/solution.py
+++ b/solution.py
@@ -13,13 +13,14 @@
 
 H = 96
 W = 180
-WIDE = 768
+WP = 192
 C = 768
 HC = 384
 NB = 8
 BS = 96
 KWP = 96
 CHIPS = 16
+DEVICES = 32
 IMAGES = 16
 MESH = pl.DeviceIdType.MESH
 f32 = jnp.float32
@@ -52,26 +53,24 @@
 
 
 def to_spectrum_table(part):
-    out = np.zeros((3, 16, 2, 2, 2, 2, 2, W, 2), np.float32)
+    out = np.zeros((3, 16, 2, 2, 2, WP, 2), np.float32)
     grouped = part.reshape(2, 16, 3, 2, W).transpose(2, 1, 0, 3, 4)
-    for jj in range(2):
-        for b in range(2):
-            out[:, :, jj, b, :, :, jj, :, b] = grouped
-    out = out.reshape(3, 256, 4 * W)
-    return np.pad(out, ((0, 0), (0, 0), (0, WIDE - 4 * W)))
+    for b in range(2):
+        out[:, :, b, :, :, :W, b] = grouped
+    return out.reshape(3, 128, 2 * WP)
 
 
 def lat_tables():
     forward = latitude_parts(1.0)
     inverse = latitude_parts(-1.0)
-    ahead = np.zeros((2, 2, 2, H, 16, 6, 2, 2, 2), np.float32)
-    back = np.zeros((16, 6, 2, 2, 2, 2, 2, 2, H), np.float32)
-    split = forward.reshape(2, H, 16, 6, 2)
-    isplit = inverse.reshape(2, 16, 6, H, 2)
+    ahead = np.zeros((2, 2, 2, H, 3, 16, 2, 2, 2, 2), np.float32)
+    back = np.zeros((3, 16, 2, 2, 2, 2, 2, 2, 2, H), np.float32)
+    split = forward.reshape(2, H, 16, 2, 3, 2).transpose(0, 1, 4, 2, 3, 5)
+    isplit = inverse.reshape(2, 16, 2, 3, H, 2).transpose(3, 1, 2, 0, 5, 4)
     for b in range(2):
         for kk in range(2):
-            ahead[:, b, kk, :, :, :, b, :, kk] = split
-            back[:, :, b, :, kk, :, b, kk, :] = isplit.transpose(1, 2, 0, 4, 3)
+            ahead[:, b, kk, :, :, :, :, b, :, kk] = split
+            back[:, :, :, b, :, kk, :, b, kk, :] = isplit
     return ahead.reshape(768, 768), back.reshape(768, 768)
 
 
@@ -90,9 +89,9 @@
     x_in, c_in, kept_in, pad_in, w_one, w_two, b_one, b_two, ft_in, tt_in, lf_in, li_in,
     out_x, out_c, out_g,
     xs, fts, tts, lfs, lis, wraw, wd, kraw, keeps, brow,
-    send, got, facc, spec, hid, slope, kt, tmp, fil, dtwo, gacc, bacc,
+    send, got, back, home, facc, spec, hid, slope, kt, tmp, fil, dtwo, gacc, bacc,
     gp, gr, s_two, gz, s_three, fin, fy,
-    load_sem, xown, xin_send, xin_recv, ssem, rsem, oloc, osend, orecv, gsend, grecv, gloc,
+    load_sem, xin, kept_sem, ssem, rsem, oloc, gsend, grecv, gloc,
 ):
     me = lax.axis_index("space")
     dp = lax.axis_index("dp")
@@ -106,48 +105,11 @@
     depth = zh * 4 + z
     buddy = (dp, 2 * m + other)
 
-    def tile(which, l):
-        return pl.ds(pl.multiple_of(which * HC + l * 128, 128), 128)
-
-    def row_slot(v, j6, l):
-        return xs.at[v, j6 // 2, l, pl.ds(lax.rem(j6, 2) * W, W)]
-
-    def row_slots(v, j6):
-        return xs.at[v, j6 // 2, :, pl.ds(lax.rem(j6, 2) * W, W)]
-
-    def load(src, dst, at):
-        return pltpu.make_async_copy(src, dst, load_sem.at[at])
-
-    def start_own(v, ref):
-        for j in range(3):
-            for l in range(3):
-                pltpu.make_async_copy(
-                    ref.at[j, :, :, tile(core, l)], row_slot(v, 3 * core + j, l), xown.at[v, j]
-                ).start()
-
-    kept_own = load(kept_in, kraw.at[pl.ds(3 * core, 3)], 0)
-    tables = [
-        load(ft_in.at[0], fts.at[0], 1),
-        load(ft_in.at[1], fts.at[1], 2),
-        load(lf_in, lfs, 3),
-        load(w_one, wraw.at[0], 4),
-        load(w_two, wraw.at[1], 5),
-        load(li_in, lis, 6),
-        load(tt_in, tts, 7),
-    ]
-    start_own(0, x_in)
-    tables[0].start()
-    start_own(1, c_in)
-    for copy in tables[1:2] + [kept_own] + tables[2:]:
-        copy.start()
-
-    barrier = pltpu.get_barrier_semaphore()
-
     def greet(device):
         pl.semaphore_signal(barrier, inc=1, device_id=device, device_id_type=MESH)
 
     def greet_group(i, carry):
-        greet((dp, 2 * lax.rem(m + i, CHIPS) + core))
+        greet((dp, lax.rem(me + i, DEVICES)))
         return carry
 
     def plane_device(i):
@@ -158,91 +120,139 @@
         greet(plane_device(4 * (i // 3) + lax.rem(i, 3) + 1))
         return carry
 
-    lax.fori_loop(1, CHIPS, greet_group, 0)
-    greet(buddy)
+    def load(src, dst, at):
+        return pltpu.make_async_copy(src, dst, load_sem.at[at])
+
+    def start_field(v, ref):
+        for l in range(6):
+            pltpu.make_async_copy(
+                ref.at[:, :, :, pl.ds(128 * l, 128)], xs.at[v, l, :, pl.ds(0, W)], xin.at[v]
+            ).start()
+
+    def wait_field(v):
+        whole = xs.at[v, :, :, pl.ds(0, W)]
+        pltpu.make_async_copy(whole, whole, xin.at[v]).wait()
+
+    kept_own = load(kept_in, kraw.at[pl.ds(3 * core, 3)], 0)
+    lon_table = load(ft_in, fts, 1)
+    tables = [
+        load(lf_in, lfs, 2),
+        load(w_one, wraw.at[0], 3),
+        load(w_two, wraw.at[1], 4),
+        load(li_in, lis, 5),
+        load(tt_in, tts, 6),
+    ]
+    start_field(0, x_in)
+    lon_table.start()
+    start_field(1, c_in)
+
+    barrier = pltpu.get_barrier_semaphore()
+    lax.fori_loop(1, DEVICES, greet_group, 0)
     lax.fori_loop(0, 12, greet_plane, 0)
     for i in range(4):
         greet((lax.rem(dp + 4, 8), 2 * (y * 4 + lax.rem(z + i, 4)) + core))
-    pl.semaphore_wait(barrier, 15 + 1 + 12 + 4)
-
-    def swap(v, ref):
-        for j in range(3):
-            for l in range(3):
-                pltpu.make_async_remote_copy(
-                    src_ref=ref.at[j, :, :, tile(other, l)],
-                    dst_ref=row_slot(v, 3 * core + j, l),
-                    send_sem=xin_send.at[v, j],
-                    recv_sem=xin_recv.at[v, j],
-                    device_id=buddy,
-                    device_id_type=MESH,
-                ).start()
+
+    for copy in [kept_own] + tables:
+        copy.start()
+    xs[:, :, :, W:] = jnp.zeros((2, 6, 3, WP - W, 2, 128), bf16)
 
     kept_swap = pltpu.make_async_remote_copy(
         src_ref=kept_in,
         dst_ref=kraw.at[pl.ds(3 * core, 3)],
-        send_sem=xin_send.at[2, 0],
-        recv_sem=xin_recv.at[2, 0],
+        send_sem=kept_sem.at[0],
+        recv_sem=kept_sem.at[1],
         device_id=buddy,
         device_id_type=MESH,
     )
-    swap(0, x_in)
-    swap(1, c_in)
-    kept_swap.start()
-    xs[:, :, :, 2 * W :] = jnp.zeros((2, 3, 3, WIDE // 2 - 2 * W, 2, 128), bf16)
-
-    def row_valid(j6):
-        return jnp.where(6 * m + j6 < H - pad_in[0], 1.0, 0.0).astype(f32)
-
-    def field(v, t):
-        return jnp.concatenate([xs.at[v, t, l].reshape(WIDE, 128)[...] for l in range(3)], axis=1)
-
-    def send_chunk(phase, a, first=1, last=CHIPS, beside=None):
+
+    def row_valid(j):
+        return jnp.where(3 * me + j < H - pad_in[0], 1.0, 0.0).astype(f32)
+
+    def transform(v, a):
+        for j in range(3):
+            field = jnp.concatenate(
+                [xs.at[v, l, j].reshape(2 * WP, 128)[...] for l in range(6)], axis=1
+            )
+            result = (dot(fts[v, a], field) * row_valid(j)).astype(bf16)
+            for l in range(6):
+                send.at[v, a, l, j].reshape(128, 128)[...] = result[:, 128 * l : 128 * l + 128]
+
+    def message(source, target, device, send_at, recv_at):
+        pltpu.make_async_remote_copy(
+            src_ref=source,
+            dst_ref=target,
+            send_sem=send_at,
+            recv_sem=recv_at,
+            device_id=device,
+            device_id_type=MESH,
+        ).start()
+
+    def send_chunk(v, a):
         def one(i, carry):
-            peer = lax.rem(m + i, CHIPS)
-            pltpu.make_async_remote_copy(
-                src_ref=send.at[phase, a, peer],
-                dst_ref=got.at[phase, a, m],
-                send_sem=ssem.at[phase, a],
-                recv_sem=rsem.at[phase, a],
-                device_id=(dp, 2 * peer + core),
-                device_id_type=MESH,
-            ).start()
+            peer = lax.rem(me + i, DEVICES)
+            pm, pc = peer // 2, lax.rem(peer, 2)
+            message(
+                send.at[v, a, pl.ds(3 * pc, 3), :, pm],
+                got.at[v, a, :, :, m, core],
+                (dp, peer),
+                ssem.at[v, a, lax.rem(pc + core, 2)],
+                rsem.at[v, a],
+            )
+            return carry
+
+        lax.fori_loop(1, DEVICES, one, 0)
+        pltpu.make_async_copy(
+            send.at[v, a, pl.ds(3 * core, 3), :, m], got.at[v, a, :, :, m, core], rsem.at[v, a]
+        ).start()
+
+    def send_back(v, a, first=1, last=DEVICES, beside=None):
+        def one(i, carry):
+            peer = lax.rem(me + i, DEVICES)
+            pm, pc = peer // 2, lax.rem(peer, 2)
+            message(
+                back.at[v, a, :, :, pm, pc],
+                home.at[v, a, pl.ds(3 * core, 3), :, m],
+                (dp, peer),
+                ssem.at[2 + v, a, lax.rem(pc + core, 2)],
+                rsem.at[2 + v, a],
+            )
             if beside is not None:
                 beside(i)
             return carry
 
         lax.fori_loop(first, last, one, 0)
-
-    def wait_chunk(phase, a, sem):
-        whole = got.at[phase, a, pl.ds(0, 15)]
-        pltpu.make_async_copy(whole, whole, sem.at[phase, a]).wait()
-
-    def to_spectrum(v):
-        line = lax.broadcasted_iota(jnp.int32, (256, HC), 0)
-        second = lax.rem(line // 8, 2) == 1
-
-        def one(a, carry):
-            for t in range(3):
-                result = dot(fts[v, a], field(v, t))
-                result = result * jnp.where(second, row_valid(2 * t + 1), row_valid(2 * t))
-                send[v, a, :, 16 * t : 16 * t + 16, :] = result.astype(bf16).reshape(16, 16, HC)
-            send_chunk(v, a)
-            got[v, a, m] = send[v, a, m]
-            return carry
-
-        lax.fori_loop(0, 3, one, 0)
-
-    for v in range(2):
-        for j in range(3):
-            here, there = row_slots(v, 3 * core + j), row_slots(v, 3 * other + j)
-            pltpu.make_async_copy(here, here, xown.at[v, j]).wait()
-            pltpu.make_async_copy(there, there, xin_recv.at[v, j]).wait()
-        tables[v].wait()
-        to_spectrum(v)
+        if last == DEVICES:
+            pltpu.make_async_copy(
+                back.at[v, a, :, :, m, core],
+                home.at[v, a, pl.ds(3 * core, 3), :, m],
+                rsem.at[2 + v, a],
+            ).start()
+
+    def wait_chunk(v, a):
+        pltpu.make_async_copy(got.at[v, a], got.at[v, a], rsem.at[v, a]).wait()
+
+    def wait_home(v, a):
+        pltpu.make_async_copy(home.at[v, a], home.at[v, a], rsem.at[2 + v, a]).wait()
+
+    wait_field(0)
+    lon_table.wait()
+    transform(0, 0)
+    pl.semaphore_wait(barrier, 31 + 12 + 4)
+    send_chunk(0, 0)
+
+    def transform_and_send(i, carry):
+        transform(i // 3, lax.rem(i, 3))
+        send_chunk(i // 3, lax.rem(i, 3))
+        return carry
+
+    lax.fori_loop(1, 3, transform_and_send, 0)
+    wait_field(1)
+    lax.fori_loop(3, 6, transform_and_send, 0)
+    kept_swap.start()
 
     gacc[...] = jnp.zeros_like(gacc)
     bacc[...] = jnp.zeros_like(bacc)
-    for copy in [kept_own, kept_swap] + tables[2:]:
+    for copy in [kept_own, kept_swap] + tables:
         copy.wait()
     lane = lax.broadcasted_iota(jnp.int32, (BS, HC), 1)
     line = lax.broadcasted_iota(jnp.int32, (BS, HC), 0)
@@ -280,14 +290,15 @@
             brow[mat, p] = jnp.where(spread, copies, 0.0).sum(0, keepdims=True)
 
     def spectral(phase, a, half):
-        held = got[phase, a].reshape(768, HC)
+        held = jnp.concatenate([got.at[phase, a, l].reshape(768, 128)[...] for l in range(3)], axis=1)
         return dot(lfs[half * HC : half * HC + HC, :], held)
 
-    def unspectral(phase, a):
+    def unspectral(v, a):
         for t in range(2):
-            result = dot(lis[t * HC : t * HC + HC, :], fil[...]).astype(bf16)
-            send[phase, a, 8 * t : 8 * t + 8] = result.reshape(8, 48, HC)
-        got[phase, a, m] = send[phase, a, m]
+            rows = slice(t * HC, t * HC + HC)
+            result = dot(lis[rows, :], fil[...]).astype(bf16)
+            for l in range(3):
+                back.at[v, a, l].reshape(768, 128)[rows, :] = result[:, 128 * l : 128 * l + 128]
 
     def product(left, mat):
         for n in range(3):
@@ -311,7 +322,7 @@
         return keeps[2 * a + kk, pl.ds(q, 32), :].astype(f32)
 
     def forward(a, carry):
-        wait_chunk(0, a, rsem)
+        wait_chunk(0, a)
         for p in range(2):
             spec[a, :, p * HC : p * HC + HC] = spectral(0, a, p).astype(bf16)
         product(spec[a], 0)
@@ -341,12 +352,12 @@
             return carry
 
         lax.fori_loop(0, 12, shrink_rows, 0)
-        unspectral(2, a)
+        unspectral(0, a)
         return carry
 
     lax.fori_loop(0, 3, forward, 0)
-    send_chunk(2, 0)
-    send_chunk(2, 1, 1, 8)
+    send_back(0, 0)
+    send_back(0, 1, 1, 16)
 
     def add_grad(mat, left, right):
         for n in range(3):
@@ -356,7 +367,7 @@
             )
 
     def backward(a, carry):
-        wait_chunk(1, a, rsem)
+        wait_chunk(1, a)
         for p in range(2):
             tmp[:, p * HC : p * HC + HC] = spectral(1, a, p)
 
@@ -380,7 +391,7 @@
         product_turned(dtwo[...], 0)
         for p in range(2):
             fil[p * HC : p * HC + HC, :] = tmp[:, p * HC : p * HC + HC].astype(bf16)
-        unspectral(3, a)
+        unspectral(1, a)
         return carry
 
     lax.fori_loop(0, 3, backward, 0)
@@ -407,19 +418,9 @@
                 summed = align(bacc[mat, :, part]).sum(0, keepdims=True)
                 gp[n, 2 * mat + p, BS:, :] = jnp.where(first_row, summed, 0.0).astype(bf16)
 
-    def message(i, source, target, device, at):
-        pltpu.make_async_remote_copy(
-            src_ref=source,
-            dst_ref=target,
-            send_sem=gsend.at[at],
-            recv_sem=grecv.at[at],
-            device_id=device,
-            device_id_type=MESH,
-        ).start()
-
     def to_depths(source, target, at):
         def one(i, carry):
-            message(i, source(i), target, depth_device(i), at)
+            message(source(i), target, depth_device(i), gsend.at[at], grecv.at[at])
             return carry
 
         lax.fori_loop(1, 8, one, 0)
@@ -439,110 +440,87 @@
 
     def to_owner(i):
         row, column = lax.rem(y + i // 4, 4), lax.rem(x + lax.rem(i, 4), 4)
-        message(i, gp.at[row, column], gr.at[4 * y + x], plane_device(i), 0)
+        message(gp.at[row, column], gr.at[4 * y + x], plane_device(i), gsend.at[0], grecv.at[0])
 
     def from_owner(i):
-        message(i, fy.at[y, x], fy.at[y, x], plane_device(i), 3)
-
-    lax.fori_loop(1, 8, lambda i, carry: (to_owner(i), carry)[1], 0)
-    send_chunk(2, 1, 8, CHIPS, to_owner)
-    send_chunk(2, 2)
+        message(fy.at[y, x], fy.at[y, x], plane_device(i), gsend.at[3], grecv.at[3])
+
+    send_back(0, 1, 16, 31, lambda i: to_owner(i - 15))
+    send_back(0, 1, 31)
+    send_back(0, 2)
     gr[4 * y + x] = gp[y, x]
     settle(gr.at[pl.ds(0, 15)], 0)
     total = gr[0].astype(f32)
     for i in range(1, 16):
         total = total + gr[i].astype(f32)
-    s_two[...] = total
+    s_two[...] = total.astype(bf16)
     to_depths(lambda i: s_two.at[depth_rows(depth_of(i))], gz.at[depth], 1)
-    send_chunk(3, 0)
+    send_back(1, 0)
     gz[depth] = s_two[depth_rows(depth), :]
     settle(gz.at[pl.ds(0, 7)], 1)
-    total = gz[0]
+    total = gz[0].astype(f32)
     for i in range(1, 8):
-        total = total + gz[i]
-    s_three[...] = total * (1.0 / (IMAGES * H))
+        total = total + gz[i].astype(f32)
+    s_three[...] = (total * (1.0 / (IMAGES * H))).astype(bf16)
     to_depths(lambda i: s_three, fin.at[depth], 2)
-    send_chunk(3, 1)
+    send_back(1, 1)
     fin[depth] = s_three[...]
     settle(fin.at[pl.ds(0, 7)], 2)
-    fy[y, x] = fin[...].reshape(128, 128).astype(bf16)
-    send_chunk(3, 2, 1, CHIPS, from_owner)
+    fy[y, x] = fin[...].reshape(128, 128)
+    send_back(1, 2, 1, 16, from_owner)
+    send_back(1, 2, 16)
 
     def leave(v):
         ref = (out_x, out_c)[v]
 
-        def add(t, a):
-            piece = got[2 + v, a, :, pl.ds(pl.multiple_of(16 * t, 16), 16), :]
-            piece = piece.reshape(256, HC)
-            for n in range(4):
-                rows = slice(n * 192, n * 192 + 192)
-                facc[t, rows, :] += dot(tts[1 - v, a, rows, :], piece)
-
-        def begin(t, carry):
-            for l in range(3):
-                part = xs.at[v, t, l].reshape(WIDE, 128)[...]
-                facc[t, :, 128 * l : 128 * l + 128] = part.astype(f32)
+        def part(j, a, n):
+            piece = jnp.concatenate(
+                [home.at[v, a, l, j].reshape(128, 128)[...] for l in range(6)], axis=1
+            )
+            rows = slice(n * WP, n * WP + WP)
+            return dot(tts[1 - v, rows, 128 * a : 128 * a + 128], piece)
+
+        def begin(j, carry):
+            for l in range(6):
+                part = xs.at[v, l, j].reshape(2 * WP, 128)[...]
+                facc[j, :, 128 * l : 128 * l + 128] = part.astype(f32)
             return carry
 
         lax.fori_loop(0, 3, begin, 0)
         for a in range(2):
-            wait_chunk(2 + v, a, rsem)
-
-            def one(t, carry):
-                add(t, a)
+            wait_home(v, a)
+
+            def one(j, carry):
+                for n in range(2):
+                    facc[j, n * WP : n * WP + WP, :] += part(j, a, n)
                 return carry
 
             lax.fori_loop(0, 3, one, 0)
-        wait_chunk(2 + v, 2, rsem)
-
-        def away(j6):
-            j = j6 - 3 * other
-            for l in range(3):
-                pltpu.make_async_remote_copy(
-                    src_ref=row_slot(v, j6, l),
-                    dst_ref=ref.at[j, :, :, tile(core, l)],
-                    send_sem=osend.at[v, j],
-                    recv_sem=orecv.at[v, j],
-                    device_id=buddy,
-                    device_id_type=MESH,
+        wait_home(v, 2)
+
+        def last(j, carry):
+            scale = row_valid(j)
+            for n in range(2):
+                rows = slice(n * WP, n * WP + WP)
+                result = ((facc[j, rows, :] + part(j, 2, n)) * scale).astype(bf16)
+                for l in range(6):
+                    xs.at[v, l, j].reshape(2 * WP, 128)[rows, :] = result[
+                        :, 128 * l : 128 * l + 128
+                    ]
+            for l in range(6):
+                pltpu.make_async_copy(
+                    xs.at[v, l, j, pl.ds(0, W)],
+                    ref.at[j, :, :, pl.ds(128 * l, 128)],
+                    oloc.at[v],
                 ).start()
-
-        def stay(j6):
-            j = j6 - 3 * core
-            for l in range(3):
-                pltpu.make_async_copy(
-                    row_slot(v, j6, l), ref.at[j, :, :, tile(core, l)], oloc.at[v, j]
-                ).start()
-
-        for step in range(3):
-            t = step * core + (2 - step) * other
-            add(t, 2)
-            for jj in range(2):
-                rows = slice(jj * 2 * W, jj * 2 * W + 2 * W)
-                scale = row_valid(2 * t + jj)
-                for l in range(3):
-                    part = facc[t, rows, 128 * l : 128 * l + 128] * scale
-                    xs.at[v, t, l].reshape(WIDE, 128)[rows, :] = part.astype(bf16)
-            if step == 0:
-                away(2 * t)
-                away(2 * t + 1)
-            elif step == 1:
-                away(2 * t + other)
-                stay(2 * t + core)
-            else:
-                stay(2 * t)
-                stay(2 * t + 1)
+            return carry
+
+        lax.fori_loop(0, 3, last, 0)
 
     def left(v):
-        ref = (out_x, out_c)[v]
-        for j in range(3):
-            gone, arrived = ref.at[j, :, :, mine], ref.at[j, :, :, theirs]
-            pltpu.make_async_copy(gone, gone, oloc.at[v, j]).wait()
-            pltpu.make_async_copy(arrived, arrived, orecv.at[v, j]).wait()
-            pltpu.make_async_copy(gone, gone, osend.at[v, j]).wait()
-
-    mine = pl.ds(pl.multiple_of(core * HC, 128), HC)
-    theirs = pl.ds(pl.multiple_of(other * HC, 128), HC)
+        whole = xs.at[v, :, :, pl.ds(0, W)]
+        pltpu.make_async_copy(whole, whole, oloc.at[v]).wait()
+
     leave(0)
 
     settle(gr.at[pl.ds(0, 15)], 3)
@@ -561,14 +539,12 @@
     leave(1)
 
     def sent(i, carry):
-        wait_chunk(i // 3, lax.rem(i, 3), ssem)
+        phase, a = i // 3, lax.rem(i, 3)
+        for at, part in ((0, got.at[0, 0, :, :, pl.ds(0, 15), 0]), (1, got.at[0, 0, :, :, :, 0])):
+            pltpu.make_async_copy(part, part, ssem.at[phase, a, at]).wait()
         return carry
 
     lax.fori_loop(0, 12, sent, 0)
-    for v in range(2):
-        for j in range(3):
-            there = row_slots(v, 3 * core + j)
-            pltpu.make_async_copy(there, there, xin_send.at[v, j]).wait()
     for at, part in (
         (0, gr.at[pl.ds(0, 15)]),
         (1, gz.at[pl.ds(0, 7)]),
@@ -585,9 +561,10 @@
 def mix(x_wide, c_wide, kept, pad_rows, w_one, w_two, b_one, b_two):
     forward_lon, inverse_lon = longitude_parts()
     ahead = np.stack([to_spectrum_table(forward_lon), to_spectrum_table(inverse_lon)])
+    turned = ahead.transpose(0, 3, 1, 2).reshape(2, 2 * WP, 3 * 128)
     lf, li = lat_tables()
     as_bf16 = lambda table: jnp.asarray(table.astype(jnp.bfloat16))
-    tables = (as_bf16(ahead), as_bf16(ahead.transpose(0, 1, 3, 2)), as_bf16(lf), as_bf16(li))
+    tables = (as_bf16(ahead), as_bf16(turned), as_bf16(lf), as_bf16(li))
     anywhere = pl.BlockSpec(memory_space=pl.ANY)
     vmem = pl.BlockSpec(memory_space=pltpu.VMEM)
     dma = pltpu.SemaphoreType.DMA
@@ -605,9 +582,9 @@
         + [anywhere] * 4,
         out_specs=(anywhere, anywhere, anywhere),
         scratch_shapes=[
-            pltpu.VMEM((2, 3, 3, WIDE // 2, 2, 128), bf16),
-            pltpu.VMEM((2, 3, 256, WIDE), bf16),
-            pltpu.VMEM((2, 3, WIDE, 256), bf16),
+            pltpu.VMEM((2, 6, 3, WP, 2, 128), bf16),
+            pltpu.VMEM((2, 3, 128, 2 * WP), bf16),
+            pltpu.VMEM((2, 2 * WP, 3 * 128), bf16),
             pltpu.VMEM((768, 768), bf16),
             pltpu.VMEM((768, 768), bf16),
             pltpu.VMEM((2, 2, NB, BS, BS), bf16),
@@ -615,9 +592,11 @@
             pltpu.VMEM((6, NB, H), jnp.int32),
             pltpu.VMEM((6, H, HC), bf16),
             pltpu.VMEM((2, 2, 1, HC), f32),
-            pltpu.VMEM((4, 3, CHIPS, 48, HC), bf16),
-            pltpu.VMEM((4, 3, CHIPS, 48, HC), bf16),
-            pltpu.VMEM((3, WIDE, HC), f32),
+            pltpu.VMEM((2, 3, 6, 3, CHIPS, 4, 2, 128), bf16),
+            pltpu.VMEM((2, 3, 3, 3, CHIPS, 2, 4, 2, 128), bf16),
+            pltpu.VMEM((2, 3, 3, 3, CHIPS, 2, 4, 2, 128), bf16),
+            pltpu.VMEM((2, 3, 6, 3, CHIPS, 4, 2, 128), bf16),
+            pltpu.VMEM((3, 2 * WP, C), f32),
             pltpu.VMEM((3, HC, 768), bf16),
             pltpu.VMEM((3, HC, 768), bf16),
             pltpu.VMEM((3, HC, 768), f32),
@@ -629,20 +608,17 @@
             pltpu.VMEM((2, 8, 768), f32),
             pltpu.VMEM((4, 4, 128, 128), bf16),
             pltpu.VMEM((16, 128, 128), bf16),
-            pltpu.VMEM((128, 128), f32),
-            pltpu.VMEM((8, 16, 128), f32),
-            pltpu.VMEM((16, 128), f32),
-            pltpu.VMEM((8, 16, 128), f32),
+            pltpu.VMEM((128, 128), bf16),
+            pltpu.VMEM((8, 16, 128), bf16),
+            pltpu.VMEM((16, 128), bf16),
+            pltpu.VMEM((8, 16, 128), bf16),
             pltpu.VMEM((4, 4, 128, 128), bf16),
-            dma((8,)),
-            dma((2, 3)),
-            dma((3, 3)),
-            dma((3, 3)),
+            dma((7,)),
+            dma((2,)),
+            dma((2,)),
+            dma((4, 3, 2)),
             dma((4, 3)),
-            dma((4, 3)),
-            dma((2, 3)),
-            dma((2, 3)),
-            dma((2, 3)),
+            dma((2,)),
             dma((5,)),
             dma((5,)),
             dma,
@@ -658,14 +634,16 @@
     held, parts, weights, biases, in_sem, out_sem, g_sem,
 ):
     loads, stores = [], []
+    load_parts = pltpu.make_async_copy(g_ref, parts, g_sem.at[0])
     for v, (source, target) in enumerate(((x_ref, out_x), (c_ref, out_c))):
         for j in range(3):
             loads.append(pltpu.make_async_copy(source.at[j], held.at[v, j], in_sem.at[v, j]))
             stores.append(pltpu.make_async_copy(held.at[v, j], target.at[j], out_sem.at[v, j]))
-    load_parts = pltpu.make_async_copy(g_ref, parts, g_sem.at[0])
+            loads[-1].start()
     load_parts.start()
-    for copy in loads:
-        copy.start()
+    for load, store in zip(loads, stores):
+        load.wait()
+        store.start()
     load_parts.wait()
     for mat, (weight, bias) in enumerate(((gw_one, gb_one), (gw_two, gb_two))):
         for p in range(2):
@@ -677,9 +655,6 @@
         stores[-1].start()
         stores.append(pltpu.make_async_copy(biases.at[mat], bias, g_sem.at[3 + mat]))
         stores[-1].start()
-    for load, store in zip(loads, stores):
-        load.wait()
-        store.start()
     for store in stores:
         store.wait()
 

time: 181 us -> 174 us (0.961)
  Pallas kernels: 178 us -> 172 us
    pallas_call x1, Pallas kernels: 174 us -> 168 us  [mix(): pl.pallas_call(kernel, out_shape=(jax.ShapeDtypeStruct(x_wide.shape, bf16...]
where the time goes in v4:
time: 174 us; the launch traced here: 173 us
  Pallas kernels  172 us (99%)
    pallas_call x1, Pallas kernels, mix(): pl.pallas_call(kernel, out_shape=(jax.ShapeDtypeStruct(x_wide.shape, bf16...  168 us
    pallas_call x1, Pallas kernels, settle_outputs(): pl.pallas_call(finish, out_shape=(jax.ShapeDtypeStruct(out_x.shape, bf16)...  4.19 us

profile of v4, /device:TPU:1, one launch (start us, length us, event | category | flops | bytes accessed | tf_op | source)
XLA Modules:
  0.0 173.4 jit_solution(10020948809291130600)
XLA Ops:
  1.3 167.8 %shard_map.163 = (bf16[3,180,2,768]{3,2,1,0:T(2,128)(2,1)}, bf16[3,180,2,768]{3,2,1,0:T(2,128)(2,1)}, bf16[2,4,4,128,128]{4,3,2,1,0:T(8,128)(2,1)}) custom-call(bf16[3,180,2,768]{3,2,1,0:T(2,128)(2,1)} %bitcast.5, bf16[3,180,2,768]{3,2,1,0:T(2,128)(2,1)} %bitcast.6, s32[3,8,96]{2,1,0:T(8,128)} %bitcast.7, s32[1]{0:T(128)S(6)} %copy.18.pad_in, ...), custom_call_target="tpu_custom_call" | custom-call | tf_op jit(solution)/shard_map/pallas_call | solution.py:571
  169.1 4.2 %shard_map.164 = (bf16[3,180,2,768]{3,2,1,0:T(2,128)(2,1)}, bf16[3,180,2,768]{3,2,1,0:T(2,128)(2,1)}, f32[2,8,96,96]{3,2,1,0:T(8,128)}, f32[2,8,96]{2,1,0:T(8,12...) custom-call(bf16[3,180,2,768]{3,2,1,0:T(2,128)(2,1)} %get-tuple-element.15.x_ref, ...), custom_call_target="tpu_custom_call" | custom-call | tf_op jit(solution)/shard_map/pallas_call | solution.py:664

commit v5 on v4

--- a/solution.py
+++ b/solution.py
@@ -52,9 +52,16 @@
     return np.stack([upper, lower], 0)
 
 
+def wavenumber_slots():
+    slots = np.arange(KWP).reshape(16, 3, 2)
+    slots[15, 1] = slots[12, 2]
+    slots[12, 2] = slots[15, 2] = KWP - 1
+    return slots
+
+
 def to_spectrum_table(part):
     out = np.zeros((3, 16, 2, 2, 2, WP, 2), np.float32)
-    grouped = part.reshape(2, 16, 3, 2, W).transpose(2, 1, 0, 3, 4)
+    grouped = part[:, wavenumber_slots()].transpose(2, 1, 0, 3, 4)
     for b in range(2):
         out[:, :, b, :, :, :W, b] = grouped
     return out.reshape(3, 128, 2 * WP)
@@ -124,14 +131,15 @@
         return pltpu.make_async_copy(src, dst, load_sem.at[at])
 
     def start_field(v, ref):
-        for l in range(6):
-            pltpu.make_async_copy(
-                ref.at[:, :, :, pl.ds(128 * l, 128)], xs.at[v, l, :, pl.ds(0, W)], xin.at[v]
-            ).start()
-
-    def wait_field(v):
-        whole = xs.at[v, :, :, pl.ds(0, W)]
-        pltpu.make_async_copy(whole, whole, xin.at[v]).wait()
+        for j in range(3):
+            for l in range(6):
+                pltpu.make_async_copy(
+                    ref.at[j, :, :, pl.ds(128 * l, 128)], xs.at[v, l, j, pl.ds(0, W)], xin.at[v, j]
+                ).start()
+
+    def wait_field(v, j):
+        whole = xs.at[v, :, j, pl.ds(0, W)]
+        pltpu.make_async_copy(whole, whole, xin.at[v, j]).wait()
 
     kept_own = load(kept_in, kraw.at[pl.ds(3 * core, 3)], 0)
     lon_table = load(ft_in, fts, 1)
@@ -155,6 +163,8 @@
     for copy in [kept_own] + tables:
         copy.start()
     xs[:, :, :, W:] = jnp.zeros((2, 6, 3, WP - W, 2, 128), bf16)
+    for chip in (12, 15):
+        home[:, 2, :, :, chip] = jnp.zeros((2, 6, 3, 4, 2, 128), bf16)
 
     kept_swap = pltpu.make_async_remote_copy(
         src_ref=kept_in,
@@ -168,8 +178,10 @@
     def row_valid(j):
         return jnp.where(3 * me + j < H - pad_in[0], 1.0, 0.0).astype(f32)
 
-    def transform(v, a):
+    def transform(v, a, loading=False):
         for j in range(3):
+            if loading:
+                wait_field(v, j)
             field = jnp.concatenate(
                 [xs.at[v, l, j].reshape(2 * WP, 128)[...] for l in range(6)], axis=1
             )
@@ -187,56 +199,79 @@
             device_id_type=MESH,
         ).start()
 
+    def is_short(chip):
+        return jnp.logical_or(chip == 12, chip == 15)
+
+    def where_held(chip, a, body):
+        if isinstance(a, int) and a != 2:
+            body()
+        else:
+            pl.when(jnp.logical_or(a != 2, jnp.logical_not(is_short(chip))))(body)
+
     def send_chunk(v, a):
         def one(i, carry):
             peer = lax.rem(me + i, DEVICES)
             pm, pc = peer // 2, lax.rem(peer, 2)
-            message(
-                send.at[v, a, pl.ds(3 * pc, 3), :, pm],
-                got.at[v, a, :, :, m, core],
-                (dp, peer),
-                ssem.at[v, a, lax.rem(pc + core, 2)],
-                rsem.at[v, a],
+            where_held(
+                pm,
+                a,
+                lambda: message(
+                    send.at[v, a, pl.ds(3 * pc, 3), :, pm],
+                    got.at[v, a, :, :, m, core],
+                    (dp, peer),
+                    ssem.at[v, a, lax.rem(pc + core, 2)],
+                    rsem.at[v, a],
+                ),
             )
             return carry
 
+        def own():
+            pltpu.make_async_copy(
+                send.at[v, a, pl.ds(3 * core, 3), :, m], got.at[v, a, :, :, m, core], rsem.at[v, a]
+            ).start()
+
         lax.fori_loop(1, DEVICES, one, 0)
-        pltpu.make_async_copy(
-            send.at[v, a, pl.ds(3 * core, 3), :, m], got.at[v, a, :, :, m, core], rsem.at[v, a]
-        ).start()
+        where_held(m, a, own)
 
     def send_back(v, a, first=1, last=DEVICES, beside=None):
         def one(i, carry):
             peer = lax.rem(me + i, DEVICES)
             pm, pc = peer // 2, lax.rem(peer, 2)
-            message(
-                back.at[v, a, :, :, pm, pc],
-                home.at[v, a, pl.ds(3 * core, 3), :, m],
-                (dp, peer),
-                ssem.at[2 + v, a, lax.rem(pc + core, 2)],
-                rsem.at[2 + v, a],
+            where_held(
+                m,
+                a,
+                lambda: message(
+                    back.at[v, a, :, :, pm, pc],
+                    home.at[v, a, pl.ds(3 * core, 3), :, m],
+                    (dp, peer),
+                    ssem.at[2 + v, a, lax.rem(pc + core, 2)],
+                    rsem.at[2 + v, a],
+                ),
             )
             if beside is not None:
                 beside(i)
             return carry
 
-        lax.fori_loop(first, last, one, 0)
-        if last == DEVICES:
+        def own():
             pltpu.make_async_copy(
                 back.at[v, a, :, :, m, core],
                 home.at[v, a, pl.ds(3 * core, 3), :, m],
                 rsem.at[2 + v, a],
             ).start()
 
+        lax.fori_loop(first, last, one, 0)
+        if last == DEVICES:
+            where_held(m, a, own)
+
     def wait_chunk(v, a):
         pltpu.make_async_copy(got.at[v, a], got.at[v, a], rsem.at[v, a]).wait()
 
     def wait_home(v, a):
-        pltpu.make_async_copy(home.at[v, a], home.at[v, a], rsem.at[2 + v, a]).wait()
-
-    wait_field(0)
+        part = home.at[v, a] if a != 2 else home.at[v, a, :, :, pl.ds(0, 14)]
+        pltpu.make_async_copy(part, part, rsem.at[2 + v, a]).wait()
+
     lon_table.wait()
-    transform(0, 0)
+    transform(0, 0, True)
     pl.semaphore_wait(barrier, 31 + 12 + 4)
     send_chunk(0, 0)
 
@@ -246,9 +281,33 @@
         return carry
 
     lax.fori_loop(1, 3, transform_and_send, 0)
-    wait_field(1)
-    lax.fori_loop(3, 6, transform_and_send, 0)
+    transform(1, 0, True)
+    send_chunk(1, 0)
+    lax.fori_loop(4, 6, transform_and_send, 0)
     kept_swap.start()
+
+    def kept_moves(i):
+        return pltpu.make_async_remote_copy(
+            src_ref=kept_in.at[pl.ds(1, 2)],
+            dst_ref=kraw.at[pl.ds(6, 2)],
+            send_sem=kept_sem.at[2 + i],
+            recv_sem=kept_sem.at[4],
+            device_id=(dp, 30 + i),
+            device_id_type=MESH,
+        )
+
+    @pl.when(me == 25)
+    def _():
+        for i in range(2):
+            kept_moves(i).start()
+        for i in range(2):
+            kept_moves(i).wait_send()
+
+    @pl.when(m == 15)
+    def _():
+        moved = kraw.at[pl.ds(6, 2)]
+        pltpu.make_async_copy(moved, moved, kept_sem.at[4]).wait()
+
 
     gacc[...] = jnp.zeros_like(gacc)
     bacc[...] = jnp.zeros_like(bacc)
@@ -271,15 +330,17 @@
     block = lax.broadcasted_iota(jnp.int32, (NB, HC), 0) - 4 * core
     spread = (lane >= BS * block) & (lane < BS * block + BS)
     for slot in range(6):
-        bits = kraw[slot].astype(f32).astype(bf16)
+        moved = 2 <= slot < 4
+        bits = kraw[slot + 4 * (m // 15) if moved else slot].astype(f32).astype(bf16)
         wide = lax.dot_general(
             bits,
             jnp.where(spread, 1.0, 0.0).astype(bf16),
             (((0,), (0,)), ((), ())),
             preferred_element_type=f32,
         )
-        real_mode = jnp.where(6 * m + slot < W // 2 + 1, 1.0, 0.0).astype(f32)
-        keeps[slot] = (wide * real_mode).astype(bf16)
+        if not moved:
+            wide = wide * jnp.where(6 * m + slot < W // 2 + 1, 1.0, 0.0).astype(f32)
+        keeps[slot] = wide.astype(bf16)
     lane = lax.broadcasted_iota(jnp.int32, (BS, HC), 1)
     tiled = sum(jnp.where(lane == line + BS * n, 1.0, 0.0).astype(f32) for n in range(4))
     for mat, ref in enumerate((b_one, b_two)):
@@ -322,6 +383,10 @@
         return keeps[2 * a + kk, pl.ds(q, 32), :].astype(f32)
 
     def forward(a, carry):
+        where_held(m, a, lambda: forward_chunk(a))
+        return carry
+
+    def forward_chunk(a):
         wait_chunk(0, a)
         for p in range(2):
             spec[a, :, p * HC : p * HC + HC] = spectral(0, a, p).astype(bf16)
@@ -353,7 +418,6 @@
 
         lax.fori_loop(0, 12, shrink_rows, 0)
         unspectral(0, a)
-        return carry
 
     lax.fori_loop(0, 3, forward, 0)
     send_back(0, 0)
@@ -367,6 +431,10 @@
             )
 
     def backward(a, carry):
+        where_held(m, a, lambda: backward_chunk(a))
+        return carry
+
+    def backward_chunk(a):
         wait_chunk(1, a)
         for p in range(2):
             tmp[:, p * HC : p * HC + HC] = spectral(1, a, p)
@@ -392,7 +460,6 @@
         for p in range(2):
             fil[p * HC : p * HC + HC, :] = tmp[:, p * HC : p * HC + HC].astype(bf16)
         unspectral(1, a)
-        return carry
 
     lax.fori_loop(0, 3, backward, 0)
 
@@ -538,13 +605,26 @@
 
     leave(1)
 
-    def sent(i, carry):
-        phase, a = i // 3, lax.rem(i, 3)
-        for at, part in ((0, got.at[0, 0, :, :, pl.ds(0, 15), 0]), (1, got.at[0, 0, :, :, :, 0])):
+    def sent(phase, a, counts):
+        for at in range(2):
+            part = got.at[0, 0, :, :, pl.ds(0, counts[at]), 0]
             pltpu.make_async_copy(part, part, ssem.at[phase, a, at]).wait()
-        return carry
-
-    lax.fori_loop(0, 12, sent, 0)
+
+    for phase in range(4):
+        for a in range(2):
+            sent(phase, a, (15, 16))
+
+    @pl.when(is_short(m))
+    def _():
+        for phase in range(2):
+            sent(phase, 2, (14, 14))
+
+    @pl.when(jnp.logical_not(is_short(m)))
+    def _():
+        for phase in range(2):
+            sent(phase, 2, (13, 14))
+            sent(2 + phase, 2, (15, 16))
+
     for at, part in (
         (0, gr.at[pl.ds(0, 15)]),
         (1, gz.at[pl.ds(0, 7)]),
@@ -589,7 +669,7 @@
             pltpu.VMEM((768, 768), bf16),
             pltpu.VMEM((2, 2, NB, BS, BS), bf16),
             pltpu.VMEM((2, 768, 768), bf16),
-            pltpu.VMEM((6, NB, H), jnp.int32),
+            pltpu.VMEM((8, NB, H), jnp.int32),
             pltpu.VMEM((6, H, HC), bf16),
             pltpu.VMEM((2, 2, 1, HC), f32),
             pltpu.VMEM((2, 3, 6, 3, CHIPS, 4, 2, 128), bf16),
@@ -614,8 +694,8 @@
             pltpu.VMEM((8, 16, 128), bf16),
             pltpu.VMEM((4, 4, 128, 128), bf16),
             dma((7,)),
-            dma((2,)),
-            dma((2,)),
+            dma((2, 3)),
+            dma((5,)),
             dma((4, 3, 2)),
             dma((4, 3)),
             dma((2,)),

time: 174 us -> 171 us (0.983)
  Pallas kernels: 172 us -> 169 us
    pallas_call x1, Pallas kernels: 168 us -> 165 us  [mix(): pl.pallas_call(kernel, out_shape=(jax.ShapeDtypeStruct(x_wide.shape, bf16...]
where the time goes in v5:
time: 171 us; the launch traced here: 170 us
  Pallas kernels  169 us (99%)
    pallas_call x1, Pallas kernels, mix(): pl.pallas_call(kernel, out_shape=(jax.ShapeDtypeStruct(x_wide.shape, bf16...  165 us
    pallas_call x1, Pallas kernels, settle_outputs(): pl.pallas_call(finish, out_shape=(jax.ShapeDtypeStruct(out_x.shape, bf16)...  4.19 us

profile of v5, /device:TPU:1, one launch (start us, length us, event | category | flops | bytes accessed | tf_op | source)
XLA Modules:
  0.0 170.4 jit_solution(16250654913274279547)
XLA Ops:
  1.3 164.8 %shard_map.163 = (bf16[3,180,2,768]{3,2,1,0:T(2,128)(2,1)}, bf16[3,180,2,768]{3,2,1,0:T(2,128)(2,1)}, bf16[2,4,4,128,128]{4,3,2,1,0:T(8,128)(2,1)}) custom-call(bf16[3,180,2,768]{3,2,1,0:T(2,128)(2,1)} %bitcast.5, bf16[3,180,2,768]{3,2,1,0:T(2,128)(2,1)} %bitcast.6, s32[3,8,96]{2,1,0:T(8,128)} %bitcast.7, s32[1]{0:T(128)S(6)} %copy.18.pad_in, ...), custom_call_target="tpu_custom_call" | custom-call | tf_op jit(solution)/shard_map/pallas_call | solution.py:651
  166.1 4.2 %shard_map.164 = (bf16[3,180,2,768]{3,2,1,0:T(2,128)(2,1)}, bf16[3,180,2,768]{3,2,1,0:T(2,128)(2,1)}, f32[2,8,96,96]{3,2,1,0:T(8,128)}, f32[2,8,96]{2,1,0:T(8,12...) custom-call(bf16[3,180,2,768]{3,2,1,0:T(2,128)(2,1)} %get-tuple-element.15.x_ref, ...), custom_call_target="tpu_custom_call" | custom-call | tf_op jit(solution)/shard_map/pallas_call | solution.py:744

commit v6 on v5

--- a/solution.py
+++ b/solution.py
@@ -94,11 +94,11 @@
 
 def kernel(
     x_in, c_in, kept_in, pad_in, w_one, w_two, b_one, b_two, ft_in, tt_in, lf_in, li_in,
-    out_x, out_c, out_g,
-    xs, fts, tts, lfs, lis, wraw, wd, kraw, keeps, brow,
+    xs, out_g,
+    fts, tts, lfs, lis, wraw, wd, kraw, keeps, brow,
     send, got, back, home, facc, spec, hid, slope, kt, tmp, fil, dtwo, gacc, bacc,
     gp, gr, s_two, gz, s_three, fin, fy,
-    load_sem, xin, kept_sem, ssem, rsem, oloc, gsend, grecv, gloc,
+    load_sem, xin, kept_sem, ssem, rsem, gsend, grecv, gloc,
 ):
     me = lax.axis_index("space")
     dp = lax.axis_index("dp")
@@ -538,8 +538,6 @@
     send_back(1, 2, 16)
 
     def leave(v):
-        ref = (out_x, out_c)[v]
-
         def part(j, a, n):
             piece = jnp.concatenate(
                 [home.at[v, a, l, j].reshape(128, 128)[...] for l in range(6)], axis=1
@@ -574,19 +572,9 @@
                     xs.at[v, l, j].reshape(2 * WP, 128)[rows, :] = result[
                         :, 128 * l : 128 * l + 128
                     ]
-            for l in range(6):
-                pltpu.make_async_copy(
-                    xs.at[v, l, j, pl.ds(0, W)],
-                    ref.at[j, :, :, pl.ds(128 * l, 128)],
-                    oloc.at[v],
-                ).start()
             return carry
 
         lax.fori_loop(0, 3, last, 0)
-
-    def left(v):
-        whole = xs.at[v, :, :, pl.ds(0, W)]
-        pltpu.make_async_copy(whole, whole, oloc.at[v]).wait()
 
     leave(0)
 
@@ -632,8 +620,6 @@
         (3, gr.at[pl.ds(0, 15)]),
     ):
         pltpu.make_async_copy(part, part, gsend.at[at]).wait()
-    left(0)
-    left(1)
     fy_away.wait()
     fy_stays.wait()
 
@@ -651,8 +637,7 @@
     return pl.pallas_call(
         kernel,
         out_shape=(
-            jax.ShapeDtypeStruct(x_wide.shape, bf16),
-            jax.ShapeDtypeStruct(c_wide.shape, bf16),
+            pltpu.VMEM((2, 6, 3, WP, 2, 128), bf16),
             jax.ShapeDtypeStruct((2, 4, 4, 128, 128), bf16),
         ),
         in_specs=[anywhere] * 3
@@ -660,9 +645,8 @@
         + [anywhere] * 2
         + [vmem] * 2
         + [anywhere] * 4,
-        out_specs=(anywhere, anywhere, anywhere),
+        out_specs=(vmem, anywhere),
         scratch_shapes=[
-            pltpu.VMEM((2, 6, 3, WP, 2, 128), bf16),
             pltpu.VMEM((2, 3, 128, 2 * WP), bf16),
             pltpu.VMEM((2, 2 * WP, 3 * 128), bf16),
             pltpu.VMEM((768, 768), bf16),
@@ -698,32 +682,33 @@
             dma((5,)),
             dma((4, 3, 2)),
             dma((4, 3)),
-            dma((2,)),
             dma((5,)),
             dma((5,)),
             dma,
         ],
         compiler_params=pltpu.CompilerParams(
-            collective_id=0, has_side_effects=True, vmem_limit_bytes=61 * 2**20
+            collective_id=0, has_side_effects=True, vmem_limit_bytes=56 * 2**20
         ),
     )(x_wide, c_wide, kept, pad_rows, w_one, w_two, b_one, b_two, *tables)
 
 
 def finish(
-    x_ref, c_ref, g_ref, out_x, out_c, gw_one, gb_one, gw_two, gb_two,
-    held, parts, weights, biases, in_sem, out_sem, g_sem,
+    fields, g_ref, out_x, out_c, gw_one, gb_one, gw_two, gb_two,
+    parts, weights, biases, out_sem, g_sem,
 ):
-    loads, stores = [], []
     load_parts = pltpu.make_async_copy(g_ref, parts, g_sem.at[0])
-    for v, (source, target) in enumerate(((x_ref, out_x), (c_ref, out_c))):
-        for j in range(3):
-            loads.append(pltpu.make_async_copy(source.at[j], held.at[v, j], in_sem.at[v, j]))
-            stores.append(pltpu.make_async_copy(held.at[v, j], target.at[j], out_sem.at[v, j]))
-            loads[-1].start()
     load_parts.start()
-    for load, store in zip(loads, stores):
-        load.wait()
-        store.start()
+    stores = []
+    for v, target in enumerate((out_x, out_c)):
+        for l in range(6):
+            stores.append(
+                pltpu.make_async_copy(
+                    fields.at[v, l, :, pl.ds(0, W)],
+                    target.at[:, :, :, pl.ds(128 * l, 128)],
+                    out_sem.at[v, l],
+                )
+            )
+            stores[-1].start()
     load_parts.wait()
     for mat, (weight, bias) in enumerate(((gw_one, gb_one), (gw_two, gb_two))):
         for p in range(2):
@@ -739,31 +724,30 @@
         store.wait()
 
 
-def settle_outputs(out_x, out_c, out_g):
+def settle_outputs(fields, out_g):
     anywhere = pl.BlockSpec(memory_space=pl.ANY)
+    vmem = pl.BlockSpec(memory_space=pltpu.VMEM)
     return pl.pallas_call(
         finish,
         out_shape=(
-            jax.ShapeDtypeStruct(out_x.shape, bf16),
-            jax.ShapeDtypeStruct(out_c.shape, bf16),
+            jax.ShapeDtypeStruct((3, W, 2, C), bf16),
+            jax.ShapeDtypeStruct((3, W, 2, C), bf16),
             jax.ShapeDtypeStruct((2, NB, BS, BS), f32),
             jax.ShapeDtypeStruct((2, NB, BS), f32),
             jax.ShapeDtypeStruct((2, NB, BS, BS), f32),
             jax.ShapeDtypeStruct((2, NB, BS), f32),
         ),
-        in_specs=[anywhere] * 3,
+        in_specs=[vmem, anywhere],
         out_specs=(anywhere,) * 6,
         scratch_shapes=[
-            pltpu.VMEM((2,) + out_x.shape, bf16),
             pltpu.VMEM(out_g.shape, bf16),
             pltpu.VMEM((2, 2, NB, BS, BS), f32),
             pltpu.VMEM((2, 2, NB, BS), f32),
-            pltpu.SemaphoreType.DMA((2, 3)),
-            pltpu.SemaphoreType.DMA((2, 3)),
+            pltpu.SemaphoreType.DMA((2, 6)),
             pltpu.SemaphoreType.DMA((5,)),
         ],
-        compiler_params=pltpu.CompilerParams(vmem_limit_bytes=60 * 2**20),
-    )(out_x, out_c, out_g)
+        compiler_params=pltpu.CompilerParams(vmem_limit_bytes=56 * 2**20),
+    )(pltpu.with_memory_space_constraint(fields, pltpu.VMEM), out_g)
 
 
 def on_device(inputs, cotangent, kept_modes, pad_rows, weight_one, bias_one, weight_two, bias_two):

time: 171 us -> 169 us (0.988)
  Pallas kernels: 169 us -> 167 us
where the time goes in v6:
time: 169 us
  Pallas kernels  167 us (99%)
    pallas_call x1, Pallas kernels, mix(): pl.pallas_call(kernel, out_shape=(pltpu.VMEM((2, 6, 3, WP, 2, 128), bf16)...  164 us

profile of v6, /device:TPU:1, one launch (start us, length us, event | category | flops | bytes accessed | tf_op | source)
XLA Modules:
  0.0 168.7 jit_solution(14081803200454389625)
XLA Ops:
  1.3 164.0 %shard_map.163 = (bf16[2,6,3,192,2,128]{5,4,3,2,1,0:T(2,128)(2,1)S(1)}, bf16[2,4,4,128,128]{4,3,2,1,0:T(8,128)(2,1)}) custom-call(bf16[3,180,2,768]{3,2,1,0:T(2,128)(2,1)} %bitcast.5, bf16[3,180,2,768]{3,2,1,0:T(2,128)(2,1)} %bitcast.6, s32[3,8,96]{2,1,0:T(8,128)} %bitcast.7, s32[1]{0:T(128)S(6)} %copy.18.pad_in, bf16[2,8,96,96]{3,2,1,0:T(8,128)(2,1)} %w_one.1, ...), custom_call_target="tpu_custom_call" | custom-call | tf_op jit(solution)/shard_map/pallas_call | solution.py:637
  165.3 3.3 %shard_map.164 = (bf16[3,180,2,768]{3,2,1,0:T(2,128)(2,1)}, bf16[3,180,2,768]{3,2,1,0:T(2,128)(2,1)}, f32[2,8,96,96]{3,2,1,0:T(8,128)}, f32[2,8,96]{2,1,0:T(8,12...) custom-call(bf16[2,6,3,192,2,128]{5,4,3,2,1,0:T(2,128)(2,1)S(1)} %get-tuple-element.14.fields, ...), custom_call_target="tpu_custom_call" | custom-call | tf_op jit(solution)/shard_map/pallas_call | solution.py:730

commit v7 on v6

--- a/solution.py
+++ b/solution.py
@@ -127,6 +127,12 @@
         greet(plane_device(4 * (i // 3) + lax.rem(i, 3) + 1))
         return carry
 
+    barrier = pltpu.get_barrier_semaphore()
+    lax.fori_loop(1, DEVICES, greet_group, 0)
+    lax.fori_loop(0, 12, greet_plane, 0)
+    for i in range(4):
+        greet((lax.rem(dp + 4, 8), 2 * (y * 4 + lax.rem(z + i, 4)) + core))
+
     def load(src, dst, at):
         return pltpu.make_async_copy(src, dst, load_sem.at[at])
 
@@ -150,16 +156,10 @@
         load(li_in, lis, 5),
         load(tt_in, tts, 6),
     ]
+    lon_table.start()
     start_field(0, x_in)
-    lon_table.start()
+
     start_field(1, c_in)
-
-    barrier = pltpu.get_barrier_semaphore()
-    lax.fori_loop(1, DEVICES, greet_group, 0)
-    lax.fori_loop(0, 12, greet_plane, 0)
-    for i in range(4):
-        greet((lax.rem(dp + 4, 8), 2 * (y * 4 + lax.rem(z + i, 4)) + core))
-
     for copy in [kept_own] + tables:
         copy.start()
     xs[:, :, :, W:] = jnp.zeros((2, 6, 3, WP - W, 2, 128), bf16)
@@ -530,12 +530,13 @@
         total = total + gz[i].astype(f32)
     s_three[...] = (total * (1.0 / (IMAGES * H))).astype(bf16)
     to_depths(lambda i: s_three, fin.at[depth], 2)
-    send_back(1, 1)
+    send_back(1, 1, 1, 16)
     fin[depth] = s_three[...]
     settle(fin.at[pl.ds(0, 7)], 2)
     fy[y, x] = fin[...].reshape(128, 128)
-    send_back(1, 2, 1, 16, from_owner)
-    send_back(1, 2, 16)
+    send_back(1, 1, 16, 31, lambda i: from_owner(i - 15))
+    send_back(1, 1, 31)
+    send_back(1, 2)
 
     def leave(v):
         def part(j, a, n):
@@ -638,14 +639,14 @@
         kernel,
         out_shape=(
             pltpu.VMEM((2, 6, 3, WP, 2, 128), bf16),
-            jax.ShapeDtypeStruct((2, 4, 4, 128, 128), bf16),
+            pltpu.VMEM((2, 4, 4, 128, 128), bf16),
         ),
         in_specs=[anywhere] * 3
         + [pl.BlockSpec(memory_space=pltpu.SMEM)]
         + [anywhere] * 2
         + [vmem] * 2
         + [anywhere] * 4,
-        out_specs=(vmem, anywhere),
+        out_specs=(vmem, vmem),
         scratch_shapes=[
             pltpu.VMEM((2, 3, 128, 2 * WP), bf16),
             pltpu.VMEM((2, 2 * WP, 3 * 128), bf16),
@@ -693,11 +694,9 @@
 
 
 def finish(
-    fields, g_ref, out_x, out_c, gw_one, gb_one, gw_two, gb_two,
-    parts, weights, biases, out_sem, g_sem,
+    fields, parts, out_x, out_c, gw_one, gb_one, gw_two, gb_two,
+    weights, biases, out_sem, g_sem,
 ):
-    load_parts = pltpu.make_async_copy(g_ref, parts, g_sem.at[0])
-    load_parts.start()
     stores = []
     for v, target in enumerate((out_x, out_c)):
         for l in range(6):
@@ -709,16 +708,15 @@
                 )
             )
             stores[-1].start()
-    load_parts.wait()
     for mat, (weight, bias) in enumerate(((gw_one, gb_one), (gw_two, gb_two))):
         for p in range(2):
             for n in range(NB):
                 block = parts[n // 4, n % 4, 2 * mat + p].astype(f32)
                 weights[mat, p, n] = block[:BS, :BS]
                 biases[mat, p, n : n + 1, :] = block[BS : BS + 1, :BS]
-        stores.append(pltpu.make_async_copy(weights.at[mat], weight, g_sem.at[1 + mat]))
+        stores.append(pltpu.make_async_copy(weights.at[mat], weight, g_sem.at[mat]))
         stores[-1].start()
-        stores.append(pltpu.make_async_copy(biases.at[mat], bias, g_sem.at[3 + mat]))
+        stores.append(pltpu.make_async_copy(biases.at[mat], bias, g_sem.at[2 + mat]))
         stores[-1].start()
     for store in stores:
         store.wait()
@@ -737,17 +735,19 @@
             jax.ShapeDtypeStruct((2, NB, BS, BS), f32),
             jax.ShapeDtypeStruct((2, NB, BS), f32),
         ),
-        in_specs=[vmem, anywhere],
+        in_specs=[vmem, vmem],
         out_specs=(anywhere,) * 6,
         scratch_shapes=[
-            pltpu.VMEM(out_g.shape, bf16),
             pltpu.VMEM((2, 2, NB, BS, BS), f32),
             pltpu.VMEM((2, 2, NB, BS), f32),
             pltpu.SemaphoreType.DMA((2, 6)),
-            pltpu.SemaphoreType.DMA((5,)),
+            pltpu.SemaphoreType.DMA((4,)),
         ],
         compiler_params=pltpu.CompilerParams(vmem_limit_bytes=56 * 2**20),
-    )(pltpu.with_memory_space_constraint(fields, pltpu.VMEM), out_g)
+    )(
+        pltpu.with_memory_space_constraint(fields, pltpu.VMEM),
+        pltpu.with_memory_space_constraint(out_g, pltpu.VMEM),
+    )
 
 
 def on_device(inputs, cotangent, kept_modes, pad_rows, weight_one, bias_one, weight_two, bias_two):

time: 169 us -> 168 us (level)
  no operation moved by 1% of the time
where the time goes in v7:
time: 168 us
  Pallas kernels  166 us (99%)
    pallas_call x1, Pallas kernels, mix(): pl.pallas_call(kernel, out_shape=(pltpu.VMEM((2, 6, 3, WP, 2, 128), bf16)...  164 us

profile of v7, /device:TPU:1, one launch (start us, length us, event | category | flops | bytes accessed | tf_op | source)
XLA Modules:
  0.0 167.6 jit_solution(6468105524775281181)
XLA Ops:
  1.3 163.7 %shard_map.163 = (bf16[2,6,3,192,2,128]{5,4,3,2,1,0:T(2,128)(2,1)S(1)}, bf16[2,4,4,128,128]{4,3,2,1,0:T(8,128)(2,1)S(1)}) custom-call(bf16[3,180,2,768]{3,2,1,0:T(2,128)(2,1)} %bitcast.5, bf16[3,180,2,768]{3,2,1,0:T(2,128)(2,1)} %bitcast.6, s32[3,8,96]{2,1,0:T(8,128)} %bitcast.7, s32[1]{0:T(128)S(6)} %copy.18.pad_in, bf16[2,8,96,96]{3,2,1,0:T(8,128)(2,1)} %w_one.1, ...), custom_call_target="tpu_custom_call" | custom-call | tf_op jit(solution)/shard_map/pallas_call | solution.py:638
  165.0 2.4 %shard_map.164 = (bf16[3,180,2,768]{3,2,1,0:T(2,128)(2,1)}, bf16[3,180,2,768]{3,2,1,0:T(2,128)(2,1)}, f32[2,8,96,96]{3,2,1,0:T(8,128)}, f32[2,8,96]{2,1,0:T(8,12...) custom-call(bf16[2,6,3,192,2,128]{5,4,3,2,1,0:T(2,128)(2,1)S(1)} %get-tuple-element.14.fields, ...), custom_call_target="tpu_custom_call" | custom-call | tf_op jit(solution)/shard_map/pallas_call | solution.py:728

commit v8 on v7

--- a/solution.py
+++ b/solution.py
@@ -421,7 +421,7 @@
 
     lax.fori_loop(0, 3, forward, 0)
     send_back(0, 0)
-    send_back(0, 1, 1, 16)
+    send_back(0, 1)
 
     def add_grad(mat, left, right):
         for n in range(3):
@@ -512,9 +512,8 @@
     def from_owner(i):
         message(fy.at[y, x], fy.at[y, x], plane_device(i), gsend.at[3], grecv.at[3])
 
-    send_back(0, 1, 16, 31, lambda i: to_owner(i - 15))
-    send_back(0, 1, 31)
-    send_back(0, 2)
+    send_back(0, 2, 1, 16, to_owner)
+    send_back(0, 2, 16)
     gr[4 * y + x] = gp[y, x]
     settle(gr.at[pl.ds(0, 15)], 0)
     total = gr[0].astype(f32)
@@ -534,9 +533,9 @@
     fin[depth] = s_three[...]
     settle(fin.at[pl.ds(0, 7)], 2)
     fy[y, x] = fin[...].reshape(128, 128)
-    send_back(1, 1, 16, 31, lambda i: from_owner(i - 15))
-    send_back(1, 1, 31)
-    send_back(1, 2)
+    send_back(1, 1, 16)
+    send_back(1, 2, 1, 16, from_owner)
+    send_back(1, 2, 16)
 
     def leave(v):
         def part(j, a, n):

time: 168 us -> 170 us (1.012)
  Pallas kernels: 166 us -> 168 us
    pallas_call x1, Pallas kernels: 164 us -> 166 us  [mix(): pl.pallas_call(kernel, out_shape=(pltpu.VMEM((2, 6, 3, WP, 2, 128), bf16)...]
where the time goes in v8:
time: 170 us
  Pallas kernels  168 us (99%)
    pallas_call x1, Pallas kernels, mix(): pl.pallas_call(kernel, out_shape=(pltpu.VMEM((2, 6, 3, WP, 2, 128), bf16)...  166 us

profile of v8, /device:TPU:1, one launch (start us, length us, event | category | flops | bytes accessed | tf_op | source)
XLA Modules:
  0.0 169.8 jit_solution(3591186050413213114)
XLA Ops:
  1.3 166.0 %shard_map.163 = (bf16[2,6,3,192,2,128]{5,4,3,2,1,0:T(2,128)(2,1)S(1)}, bf16[2,4,4,128,128]{4,3,2,1,0:T(8,128)(2,1)S(1)}) custom-call(bf16[3,180,2,768]{3,2,1,0:T(2,128)(2,1)} %bitcast.5, bf16[3,180,2,768]{3,2,1,0:T(2,128)(2,1)} %bitcast.6, s32[3,8,96]{2,1,0:T(8,128)} %bitcast.7, s32[1]{0:T(128)S(6)} %copy.18.pad_in, bf16[2,8,96,96]{3,2,1,0:T(8,128)(2,1)} %w_one.1, ...), custom_call_target="tpu_custom_call" | custom-call | tf_op jit(solution)/shard_map/pallas_call | solution.py:637
  167.3 2.4 %shard_map.164 = (bf16[3,180,2,768]{3,2,1,0:T(2,128)(2,1)}, bf16[3,180,2,768]{3,2,1,0:T(2,128)(2,1)}, f32[2,8,96,96]{3,2,1,0:T(8,128)}, f32[2,8,96]{2,1,0:T(8,12...) custom-call(bf16[2,6,3,192,2,128]{5,4,3,2,1,0:T(2,128)(2,1)S(1)} %get-tuple-element.14.fields, ...), custom_call_target="tpu_custom_call" | custom-call | tf_op jit(solution)/shard_map/pallas_call | solution.py:727
